TPU v7x, 512 devices: a whole 4x4x16 slice. The times are simulated.
512 devices in a mesh: mesh: 128 (over z, x, core), col: 4 (over y).
Axes of the slice: x: 4, y: 4, z: 16, core: 2. Of those that a mesh axis runs over, the one named last changes fastest.
Arguments:
- x_cols: bfloat16 [32, 131072], P('col', 'mesh'), may hold values from -6 to 6
- q_tiles: bfloat16 [5120, 128, 128], P('mesh'), may hold values from -0.25 to 0.25
- q_cols: int32 [1024, 5], P('mesh'), may hold values from 0 to 15, as said below
- halo_ids: int32 [128, 2], P('mesh'), may hold values from 0 to 7
- a_tiles: bfloat16 [8192, 128, 128], P('mesh'), may hold values from -0.1875 to 0.1875
- obs_prec: bfloat16 [8192, 128], P('mesh'), may hold values from 0.5 to 4
- tile_owner: int32 [8192, 1], P('mesh'), may hold values from 0 to 127; in each aligned block of 64 rows (0 to 63, 64 to 127, ...) at most 2 rows name the same one
- tile_sub: int32 [8192], P('mesh'), may hold values from 0 to 7
Outputs:
- product: float32 [32, 131072], P('col', 'mesh')
- gram: float32 [32, 32], P(None, 'col')
Inputs may be any that keep to these rules, and one draw needn't show every extreme that they name: `q_cols`: slot values index a partition's window of 16 row blocks as the first step defines. `tile_owner`: among the 64 tiles of one partition, no partition is named more than 2 times.
All inputs are finite; a program needn't handle non-finite values.
Results may differ from a plain program's by a relative error of at most 0.00081.
Values may be sent and summed in bfloat16 or wider, within the bound.
A program may use at most 64 MiB of HBM per device.

v0:
```python
import math

import jax
import jax.numpy as jnp
from jax import lax
from jax.sharding import Mesh
from jax.sharding import PartitionSpec as P

MESH = ("mesh_0", "mesh_1", "mesh_2")


HIGHEST = lax.Precision.HIGHEST


def laid_out(tiles, dim):
    shape = list(tiles.shape[1:])
    shape[dim] *= tiles.shape[0]
    return jnp.moveaxis(tiles, 0, dim).reshape(shape)


def sent_to_all(array, axis):
    copies = jnp.broadcast_to(array, (lax.axis_size(axis), *array.shape))
    return lax.all_to_all(copies, axis, split_axis=0, concat_axis=0, tiled=True)


def gather_directly(array, axis, dim):
    return laid_out(sent_to_all(array, axis), dim)


def passed_along(array, axis, by):
    length = lax.axis_size(axis)
    return lax.ppermute(array, axis, [(i, (i + by) % length) for i in range(length)])


def over_axes(array, axes):
    for axis in axes:
        array = lax.psum(array, axis)
    return array


def tile_terms(obs_tiles, precisions, x_tiles):
    projected = jnp.einsum("ton,tcn->tco", obs_tiles, x_tiles, preferred_element_type=jnp.float32)
    weighted = (precisions.astype(jnp.float32)[:, None, :] * projected).astype(jnp.bfloat16)
    return jnp.einsum("ton,tco->tcn", obs_tiles, weighted, preferred_element_type=jnp.float32)


def body(x_cols, q_tiles, q_cols, halo_ids, a_tiles, obs_prec, tile_owner, tile_sub):
    col_width, local_nodes = x_cols.shape
    tile_size = a_tiles.shape[1]
    row_blocks = local_nodes // tile_size
    neighbours = q_cols.shape[1]
    mesh_parts = lax.axis_size(MESH)
    obs_count = a_tiles.shape[0]
    capacity = max(2, 2 * obs_count // mesh_parts)
    slot_count = mesh_parts * capacity
    tile_total = row_blocks * neighbours
    probes = gather_directly(x_cols, "col", 0)
    blocks = x_cols.reshape(col_width, row_blocks, tile_size).transpose(1, 0, 2)
    block_ids = jnp.arange(row_blocks, dtype=jnp.int32)
    picker = (block_ids[None, :] == halo_ids[0][:, None]).astype(jnp.bfloat16)
    shared = jnp.einsum("hr,rcn->hcn", picker, blocks, preferred_element_type=jnp.float32).astype(
        jnp.bfloat16
    )
    left_far = passed_along(shared, MESH, 2)
    left_near = passed_along(shared, MESH, 1)
    right_near = passed_along(shared, MESH, -1)
    right_far = passed_along(shared, MESH, -2)
    window = jnp.concatenate([blocks, left_far, left_near, right_near, right_far], axis=0)
    slot_list = q_cols.reshape(-1)
    chosen = jnp.take(window, slot_list, axis=0)
    tile_products = jnp.einsum("kij,kcj->kci", q_tiles, chosen, preferred_element_type=jnp.float32)
    tile_rows = jnp.arange(tile_total, dtype=jnp.int32) // neighbours
    row_map = (block_ids[:, None] == tile_rows[None, :]).astype(jnp.float32)
    prior_part = jnp.einsum("rk,kcn->rcn", row_map, tile_products, precision=HIGHEST)
    owners = tile_owner[:, 0]
    positions = jnp.arange(obs_count, dtype=jnp.int32)
    earlier = (owners[:, None] == owners[None, :]) & (positions[None, :] < positions[:, None])
    rank_of = jnp.sum(earlier.astype(jnp.int32), axis=1)
    slot_of = owners * capacity + rank_of
    slot_ids = jnp.arange(slot_count, dtype=jnp.int32)
    placed = slot_ids[:, None] == slot_of[None, :]
    asked_ids = jnp.sum(jnp.where(placed, tile_sub[None, :] + 1, 0), axis=1) - 1
    source_tile = jnp.sum(jnp.where(placed, positions[None, :], 0), axis=1)
    incoming = lax.all_to_all(asked_ids, MESH, split_axis=0, concat_axis=0, tiled=True)
    landing = block_ids[:, None] == incoming[None, :]
    answer = jnp.einsum(
        "rs,rcn->scn", landing.astype(jnp.bfloat16), blocks, preferred_element_type=jnp.float32
    ).astype(jnp.bfloat16)
    x_tiles = lax.all_to_all(answer, MESH, split_axis=0, concat_axis=0, tiled=True)
    sent_terms = tile_terms(
        jnp.take(a_tiles, source_tile, axis=0), jnp.take(obs_prec, source_tile, axis=0), x_tiles
    )
    slot_terms = lax.all_to_all(sent_terms, MESH, split_axis=0, concat_axis=0, tiled=True)
    observed = jnp.einsum("rs,scn->rcn", landing.astype(jnp.float32), slot_terms, precision=HIGHEST)
    combined = prior_part + observed
    y_local = combined.transpose(1, 0, 2).reshape(col_width, local_nodes)
    partial_value = jnp.dot(probes.astype(jnp.float32), y_local.T, precision=HIGHEST)
    total_nodes = local_nodes * mesh_parts
    gram_block = over_axes(partial_value, MESH) / math.sqrt(total_nodes)
    return (y_local, gram_block)


def solution(mesh):
    torus = Mesh(
        mesh.devices.reshape(16, 4, 2, mesh.shape["col"]), ("mesh_0", "mesh_1", "mesh_2", "col")
    )
    in_specs = (
        P("col", MESH),
        P(MESH, None, None),
        P(MESH, None),
        P(MESH, None),
        P(MESH, None, None),
        P(MESH, None),
        P(MESH, None),
        P(MESH),
    )
    out_specs = (P("col", MESH), P(None, "col"))
    return jax.shard_map(body, mesh=torus, in_specs=in_specs, out_specs=out_specs, check_vma=False)
```

profile of v0, /device:TPU:1, one launch (start us, length us, event | category | flops | bytes accessed | tf_op | source)
XLA Modules:
  0.0 207.0 jit_solution(14219358572406026463)
XLA Ops:
  0.6 0.0 copy-start
  0.6 1.0 convert_reduce_fusion
  1.6 0.7 multiply_add_fusion
  2.3 0.1 select_reduce_fusion.1
  2.4 0.1 sub.14
  2.6 35.1 %all_to_all.21 = s32[128,2,1]{1,2,0:T(1,128)S(1)} all-to-all(s32[128,2,1]{1,2,0:T(1,128)S(1)} %bitcast.37), channel_id=1, replica_groups=mesh['mesh_0'=16,'mesh_1'=4,'mesh_2'=2,'col'=4] {'mesh_0','mesh_1','mesh..., dimensions={0} | all-to-all | bytes 2048 | tf_op jit(solution)/shard_map/all_to_all | solution.py:84
  37.7 0.5 broadcast.118
  38.2 0.8 reduce.3
  39.0 0.1 eq.83
  39.1 1.1 convolution_convert_fusion
  40.2 1.2 copy.44
  41.4 5.7 %all-to-all-start.1 = ((bf16[256,8,128]{2,1,0:T(8,128)(2,1)}), bf16[256,8,128]{2,1,0:T(8,128)(2,1)S(1)}, u32[]{:S(2)}, u32[]{:S(2)}) async-start(bf16[256,8,128]{2,1,0:T(8,128)(2,1)} %copy.44), calls=%async_computation.1 | async-start | bytes 1048576 | tf_op jit(solution)/shard_map/all_to_all | solution.py:89
  47.1 1.4 gather_fusion.1
  48.6 0.0 copy-done
  48.6 8.4 %gather_fusion.2 = bf16[256,128,128]{2,1,0:T(8,128)(2,1)} fusion(bf16[64,128,128]{2,1,0:T(8,128)(2,1)S(1)} %copy-done, s32[1024]{0:T(1024)S(1)} %pad_clamp_fusion), kind=kCustom, calls=%fused_computation.2 | custom fusion | bytes 16778240 | tf_op jit(solution)/shard_map/jit(_take)/gather | solution.py:91
  56.9 0.1 select_convert_fusion
  57.1 0.0 copy-start.1
  57.1 0.0 copy-start.4
  57.1 0.0 copy-start.3
  57.1 21.3 %all-to-all-done.1 = bf16[256,8,128]{2,1,0:T(8,128)(2,1)S(1)} async-done(((bf16[256,8,128]{2,1,0:T(8,128)(2,1)}), bf16[256,8,128]{2,1,0:T(8,128)(2,1)S(1)}, u32[]{:S(2)}, u32[]{:S(2)}) %all-to-all-start.1) | async-done | bytes 524320 | tf_op jit(solution)/shard_map/all_to_all | solution.py:89
  78.4 13.2 %fusion = f32[256,8,128]{2,1,0:T(8,128)} fusion(bf16[256,128,128]{2,1,0:T(8,128)(2,1)} %gather_fusion.2, pred[256]{0:T(512)(128)(4,1)S(1)} %compare_and_fusion, bf16[256,8,128]{2,1,0:T(8,128)(2,1)S(1)} %all-to-all-done.1, f32[256,128]{1,0:T(8,128)S(1)} %select_convert_fusion), kind=kOutput, calls=%fused_computation.4 | convolution fusion | flops 143130624 | bytes 10092800 | tf_op jit(solution)/shard_map/ton,tco->tcn/dot_general | solution.py:44
  91.6 8.8 %all-to-all-start.2 = ((f32[256,8,128]{2,1,0:T(8,128)}), f32[256,8,128]{2,1,0:T(8,128)S(1)}, u32[]{:S(2)}, u32[]{:S(2)}) async-start(f32[256,8,128]{2,1,0:T(8,128)} %fusion), calls=%async_computation.2 | async-start | bytes 2097152 | tf_op jit(solution)/shard_map/all_to_all | solution.py:93
  100.4 0.0 copy-done.1
  100.4 0.0 copy-done.4
  100.4 0.2 convolution_convert_fusion.1
  100.6 3.3 %collective-permute-start = (bf16[2,8,128]{2,0,1:T(2,128)(2,1)S(1)}, bf16[2,8,128]{2,0,1:T(2,128)(2,1)S(1)}, u32[]{:S(2)}, u32[]{:S(2)}) collective-permute-start(bf16[2,8,128]{2,0,1:T(2,128)(2,1)S(1)} %convolution_convert_fusion.1), channel_id=1, source_target_pairs={{0,8},{4,12},{8,16},{12,20},{16,24},{20,28},{24,32},{28,36},{32,40... | collective-permute-start | bytes 12296 | tf_op jit(solution)/shard_map/ppermute | solution.py:32
  103.9 3.6 %collective-permute-start.1 = (bf16[2,8,128]{2,0,1:T(2,128)(2,1)S(1)}, bf16[2,8,128]{2,0,1:T(2,128)(2,1)S(1)}, u32[]{:S(2)}, u32[]{:S(2)}) collective-permute-start(bf16[2,8,128]{2,0,1:T(2,128)(2,1)S(1)} %convolution_convert_fusion.1), channel_id=1, source_target_pairs={{0,4},{4,8},{8,12},{12,16},{16,20},{20,24},{24,28},{28,32},{32,36}... | collective-permute-start | bytes 12296 | tf_op jit(solution)/shard_map/ppermute | solution.py:32
  107.5 1.9 collective-permute-start.2
  109.4 5.5 %collective-permute-start.3 = (bf16[2,8,128]{2,0,1:T(2,128)(2,1)S(1)}, bf16[2,8,128]{2,0,1:T(2,128)(2,1)S(1)}, u32[]{:S(2)}, u32[]{:S(2)}) collective-permute-start(bf16[2,8,128]{2,0,1:T(2,128)(2,1)S(1)} %convolution_convert_fusion.1), channel_id=1, source_target_pairs={{0,504},{4,508},{8,0},{12,4},{16,8},{20,12},{24,16},{28,20},{32,24... | collective-permute-start | bytes 12296 | tf_op jit(solution)/shard_map/ppermute | solution.py:32
  115.0 0.0 copy-done.3
  115.0 0.1 reshape.126
  115.0 0.1 reshape.124
  115.2 34.0 %collective-permute-done = bf16[2,8,128]{2,0,1:T(2,128)(2,1)S(1)} collective-permute-done((bf16[2,8,128]{2,0,1:T(2,128)(2,1)S(1)}, bf16[2,8,128]{2,0,1:T(2,128)(2,1)S(1)}, u32[]{:S(2)}, u32[]{:S(2)}) %collective-permute-start) | collective-permute-done | bytes 4128 | tf_op jit(solution)/shard_map/ppermute | solution.py:32
  149.2 0.0 collective-permute-done.1
  149.2 0.0 collective-permute-done.2
  149.2 0.0 collective-permute-done.3
  149.3 0.6 gather_fusion
  149.9 2.1 %fusion.9 = f32[40,8,128]{2,1,0:T(8,128)S(1)} fusion(bf16[40,128,128]{2,1,0:T(8,128)(2,1)} %param.9, bf16[40,8,128]{2,1,0:T(8,128)(2,1)S(1)} %gather_fusion, pred[40]{0:T(512)(128)(4,1)S(1)} %compare_and_fusion.1), kind=kOutput, calls=%fused_computation.17 | convolution fusion | flops 10526720 | bytes 1556520 | tf_op jit(solution)/shard_map/kij,kcj->kci/dot_general | solution.py:71
  152.0 0.2 fusion.7
  152.2 0.0 all-to-all-done.2
  152.2 0.6 broadcast_in_dim.72
  152.9 4.2 %all-to-all-start.3 = ((bf16[4,8,1024]{2,1,0:T(8,128)(2,1)}), bf16[4,8,1024]{2,1,0:T(8,128)(2,1)S(1)}, u32[]{:S(2)}, u32[]{:S(2)}) async-start(bf16[4,8,1024]{2,1,0:T(8,128)(2,1)} %broadcast_in_dim.72), calls=%async_computation.3 | async-start | bytes 131072 | tf_op jit(solution)/shard_map/all_to_all | solution.py:23
  157.0 0.5 fusion.4
  157.6 0.0 copy-start.2
  157.6 3.9 %all-to-all-done.3 = bf16[4,8,1024]{2,1,0:T(8,128)(2,1)S(1)} async-done(((bf16[4,8,1024]{2,1,0:T(8,128)(2,1)}), bf16[4,8,1024]{2,1,0:T(8,128)(2,1)S(1)}, u32[]{:S(2)}, u32[]{:S(2)}) %all-to-all-start.3) | async-done | bytes 65568 | tf_op jit(solution)/shard_map/all_to_all | solution.py:23
  161.5 0.1 convolution_bitcast_fusion
  161.6 25.6 %psum.21 = f32[32,8]{0,1:T(8,128)S(1)} all-reduce(f32[32,8]{0,1:T(8,128)S(1)} %convolution_bitcast_fusion), channel_id=1, replica_groups=mesh['mesh_0'=16,'mesh_1'=4,'mesh_2'=2,'col'=4] {'mesh_0'}, use_global_device_ids=true, to_apply=%region_3.4 | all-reduce | flops 256 | bytes 2048 | tf_op jit(solution)/shard_map/psum | solution.py:37
  187.2 6.5 %psum.22 = f32[32,8]{0,1:T(8,128)S(1)} all-reduce(f32[32,8]{0,1:T(8,128)S(1)} %psum.21), channel_id=1, replica_groups=mesh['mesh_0'=16,'mesh_1'=4,'mesh_2'=2,'col'=4] {'mesh_1'}, use_global_device_ids=true, to_apply=%region_4.5 | all-reduce | flops 256 | bytes 2048 | tf_op jit(solution)/shard_map/psum | solution.py:37
  193.7 12.7 %psum.23 = f32[32,8]{0,1:T(8,128)S(1)} all-reduce(f32[32,8]{0,1:T(8,128)S(1)} %psum.22), channel_id=1, replica_groups=mesh['mesh_0'=16,'mesh_1'=4,'mesh_2'=2,'col'=4] {'mesh_2'}, use_global_device_ids=true, to_apply=%region_5.6 | all-reduce | flops 256 | bytes 2048 | tf_op jit(solution)/shard_map/psum | solution.py:37
  206.4 0.6 broadcast_multiply_fusion
  207.0 0.0 copy-done.2
  (14 shorter events, 0.1 us)
Async XLA Ops:
  0.6 47.9 %copy-start = (bf16[64,128,128]{2,1,0:T(8,128)(2,1)S(1)}, bf16[64,128,128]{2,1,0:T(8,128)(2,1)}, u32[]{:S(2)}) copy-start(bf16[64,128,128]{2,1,0:T(8,128)(2,1)} %param.12) | copy-start | bytes 6291460
  41.4 37.0 %all-to-all-start.1 = ((bf16[256,8,128]{2,1,0:T(8,128)(2,1)}), bf16[256,8,128]{2,1,0:T(8,128)(2,1)S(1)}, u32[]{:S(2)}, u32[]{:S(2)}) async-start(bf16[256,8,128]{2,1,0:T(8,128)(2,1)} %copy.44), calls=%async_computation.1 | async-start | bytes 1048576 | tf_op jit(solution)/shard_map/all_to_all | solution.py:89
  57.1 43.3 %copy-start.1 = (bf16[8,1024]{1,0:T(8,128)(2,1)S(1)}, bf16[8,1024]{1,0:T(8,128)(2,1)}, u32[]{:S(2)}) copy-start(bf16[8,1024]{1,0:T(8,128)(2,1)} %param.8) | copy-start | bytes 49156
  57.1 43.3 %copy-start.4 = (s32[1,2]{1,0:T(1,128)S(1)}, s32[1,2]{1,0:T(1,128)}, u32[]{:S(2)}) copy-start(s32[1,2]{1,0:T(1,128)} %param.11) | copy-start | bytes 28
  57.1 57.9 %copy-start.3 = (s32[8,5]{1,0:T(8,128)S(1)}, s32[8,5]{1,0:T(8,128)}, u32[]{:S(2)}) copy-start(s32[8,5]{1,0:T(8,128)} %param.10) | copy-start | bytes 484
  91.6 60.6 %all-to-all-start.2 = ((f32[256,8,128]{2,1,0:T(8,128)}), f32[256,8,128]{2,1,0:T(8,128)S(1)}, u32[]{:S(2)}, u32[]{:S(2)}) async-start(f32[256,8,128]{2,1,0:T(8,128)} %fusion), calls=%async_computation.2 | async-start | bytes 2097152 | tf_op jit(solution)/shard_map/all_to_all | solution.py:93
  100.6 48.6 %collective-permute-start = (bf16[2,8,128]{2,0,1:T(2,128)(2,1)S(1)}, bf16[2,8,128]{2,0,1:T(2,128)(2,1)S(1)}, u32[]{:S(2)}, u32[]{:S(2)}) collective-permute-start(bf16[2,8,128]{2,0,1:T(2,128)(2,1)S(1)} %convolution_convert_fusion.1), channel_id=1, source_target_pairs={{0,8},{4,12},{8,16},{12,20},{16,24},{20,28},{24,32},{28,36},{32,40... | collective-permute-start | bytes 12296 | tf_op jit(solution)/shard_map/ppermute | solution.py:32
  103.9 45.3 %collective-permute-start.1 = (bf16[2,8,128]{2,0,1:T(2,128)(2,1)S(1)}, bf16[2,8,128]{2,0,1:T(2,128)(2,1)S(1)}, u32[]{:S(2)}, u32[]{:S(2)}) collective-permute-start(bf16[2,8,128]{2,0,1:T(2,128)(2,1)S(1)} %convolution_convert_fusion.1), channel_id=1, source_target_pairs={{0,4},{4,8},{8,12},{12,16},{16,20},{20,24},{24,28},{28,32},{32,36}... | collective-permute-start | bytes 12296 | tf_op jit(solution)/shard_map/ppermute | solution.py:32
  107.5 41.7 %collective-permute-start.2 = (bf16[2,8,128]{2,0,1:T(2,128)(2,1)S(1)}, bf16[2,8,128]{2,0,1:T(2,128)(2,1)S(1)}, u32[]{:S(2)}, u32[]{:S(2)}) collective-permute-start(bf16[2,8,128]{2,0,1:T(2,128)(2,1)S(1)} %convolution_convert_fusion.1), channel_id=1, source_target_pairs={{0,508},{4,0},{8,4},{12,8},{16,12},{20,16},{24,20},{28,24},{32,28}... | collective-permute-start | bytes 12296 | tf_op jit(solution)/shard_map/ppermute | solution.py:32
  109.4 39.8 %collective-permute-start.3 = (bf16[2,8,128]{2,0,1:T(2,128)(2,1)S(1)}, bf16[2,8,128]{2,0,1:T(2,128)(2,1)S(1)}, u32[]{:S(2)}, u32[]{:S(2)}) collective-permute-start(bf16[2,8,128]{2,0,1:T(2,128)(2,1)S(1)} %convolution_convert_fusion.1), channel_id=1, source_target_pairs={{0,504},{4,508},{8,0},{12,4},{16,8},{20,12},{24,16},{28,20},{32,24... | collective-permute-start | bytes 12296 | tf_op jit(solution)/shard_map/ppermute | solution.py:32
  152.9 8.7 %all-to-all-start.3 = ((bf16[4,8,1024]{2,1,0:T(8,128)(2,1)}), bf16[4,8,1024]{2,1,0:T(8,128)(2,1)S(1)}, u32[]{:S(2)}, u32[]{:S(2)}) async-start(bf16[4,8,1024]{2,1,0:T(8,128)(2,1)} %broadcast_in_dim.72), calls=%async_computation.3 | async-start | bytes 131072 | tf_op jit(solution)/shard_map/all_to_all | solution.py:23
  157.6 49.4 %copy-start.2 = (f32[1,8,8,128]{3,1,2,0:T(8,128)}, f32[1,8,8,128]{3,1,2,0:T(8,128)S(1)}, u32[]{:S(2)}) copy-start(f32[1,8,8,128]{3,1,2,0:T(8,128)S(1)} %copy.60) | copy-start | bytes 98308
where the time goes:
time: 208 us; the launch traced here: 207 us
  blocking collectives  79.8 us (38%)
  waiting for transfers between devices  59.2 us (28%)
  starting transfers between devices  33 us (16%)
  matrix products  17.5 us (8%)
  local copies, waits for them, and re-layouts  13.3 us (6%)
  other arithmetic  3.34 us (2%)
    psum x3, blocking collectives, over_axes(): array = lax.psum(array, axis)  44.7 us
    all_to_all x1, blocking collectives, body(): lax.all_to_all(asked_ids, MESH, split_axis=0, concat_axis=0, tiled=True)  35.1 us
    ppermute x4, waiting for transfers between devices, passed_along(): lax.ppermute(array, axis, [(i, (i + by) % length) for i in range(length)])  34 us
    all_to_all x1, waiting for transfers between devices, body(): lax.all_to_all(answer, MESH, split_axis=0, concat_axis=0, tiled=True)  21.3 us
    ppermute x4, starting transfers between devices, passed_along(): lax.ppermute(array, axis, [(i, (i + by) % length) for i in range(length)])  14.3 us
    dot_general x1, matrix products, tile_terms(): jnp.einsum('ton,tco->tcn', obs_tiles, weighted, preferred_element_type=jn...  13.2 us
    all_to_all x1, starting transfers between devices, body(): lax.all_to_all(sent_terms, MESH, split_axis=0, concat_axis=0, tiled=True)  8.78 us
    gather x1, local copies, waits for them, and re-layouts, body(): jnp.take(a_tiles, source_tile, axis=0)  8.38 us
  transfers between devices with their start and end apart: 7, of which 3 were waited for; matrix products, arithmetic and copies ran while one was open for 7% of the time, Pallas kernels for 0%

commit v1 on v0

v1 whole, which is shorter than its diff:
```python
import functools
import math

import jax
import jax.numpy as jnp
from jax import lax
from jax.experimental import pallas as pl
from jax.experimental.pallas import tpu as pltpu
from jax.sharding import Mesh
from jax.sharding import PartitionSpec as P

LOGICAL = pl.DeviceIdType.MESH
Z, X, C, Y = 16, 4, 2, 4
PLANE = X * C
PARTS = Z * PLANE
TB = 128
COLS = 8
RB = 8
NB = 5
TILES = 64
SLOTS = 2 * Z
F32 = jnp.float32
BF16 = jnp.bfloat16
NT = (((1,), (1,)), ((), ()))
NN = (((1,), (0,)), ((), ()))


def kernel(
    x_ref, qc_ref, halo_ref, prec_ref, owner_ref, sub_ref, q_hbm, a_hbm,
    y_ref, g_ref,
    q_v, a_v, win, share, zx, xy, req, meta, req_s, meta_s, stage, xs, cb, stage2, rc, dn, zr, acc, g1, g2, gp, prec, mine,
    loc_sem, s_z, r_z, s_q, r_q, s_y, r_y, s_h, r_h, s_p, r_p, s_c, r_c, s_d, r_d, s_g1, r_g1, s_g2, r_g2,
):
    z, x, c, y = (lax.axis_index(n) for n in ("z", "x", "core", "col"))
    mq = x * C + c
    me = z * PLANE + mq

    def at_z(d):
        return {"z": lax.rem(z + d, Z)}

    def plane_peer(k):
        px, pc = lax.rem(x + k // C, X), lax.rem(c + k % C, C)
        return {"x": px, "core": pc}, px * C + pc

    def at_part(d):
        p = lax.rem(me + d + PARTS, PARTS)
        return {"z": p // PLANE, "x": lax.rem(p // C, X), "core": lax.rem(p, C)}

    def at_y(d):
        return {"col": lax.rem(y + d, Y)}

    def send(src, dst, ss, rs, where):
        return pltpu.make_async_remote_copy(
            src_ref=src, dst_ref=dst, send_sem=ss, recv_sem=rs, device_id=where, device_id_type=LOGICAL
        )

    barrier = pltpu.get_barrier_semaphore()
    halo_steps = (2, 1, -1, -2)
    others = [at_z(d) for d in range(1, Z)] + [plane_peer(k)[0] for k in range(1, PLANE)]
    others += [at_part(d) for d in halo_steps] + [at_y(d) for d in range(1, Y)]
    for other in others:
        pl.semaphore_signal(barrier, inc=1, device_id=other, device_id_type=LOGICAL)

    a_in = pltpu.make_async_copy(a_hbm, a_v, loc_sem.at[0])
    q_in = pltpu.make_async_copy(q_hbm, q_v, loc_sem.at[1])
    q_in.start()
    a_in.start()

    for r in range(RB):
        block = x_ref[:, r * TB:(r + 1) * TB]
        win[r] = block
        mine[r] = block
        zx[z, r] = block
    xy[y] = x_ref[...]
    for h in range(2):
        share[h] = mine[halo_ref[0, h]]

    prec[...] = prec_ref[...].astype(F32)
    shape = (TILES, TB)
    lane = lax.broadcasted_iota(jnp.int32, shape, 1)
    row = lax.broadcasted_iota(jnp.int32, shape, 0)
    eye = lane == row
    own_b = jnp.broadcast_to(owner_ref[...], shape)
    own_r = jnp.sum(jnp.where(eye, own_b, 0), axis=0, keepdims=True)
    sub_b = jnp.broadcast_to(jnp.sum(jnp.where(eye, sub_ref[...], 0), axis=1, keepdims=True), shape)
    same = own_b == own_r
    j_b = jnp.broadcast_to(
        jnp.sum(jnp.where(same & (lane < row), 1, 0), axis=1, keepdims=True), shape)
    j_r = jnp.sum(jnp.where(same & (row < lane), 1, 0), axis=0, keepdims=True)
    col_b = jnp.bitwise_and(own_b, PLANE - 1)
    key_b = jnp.right_shift(own_b, 3) * 2 + j_b
    for q in range(PLANE):
        hit = (col_b == q) & (key_b == lane)
        wanted = jnp.sum(jnp.where(hit, sub_b + 1, 0), axis=0, keepdims=True) - 1
        meta[q:q + 1] = wanted
        req[mq, q:q + 1] = wanted
        meta[PLANE + q:PLANE + q + 1] = jnp.sum(jnp.where(hit, row - TILES, 0), axis=0, keepdims=True) + TILES
    slot_r = jnp.bitwise_and(own_r, PLANE - 1) * SLOTS + jnp.right_shift(own_r, 3) * 2 + j_r
    meta[2 * PLANE:] = jnp.broadcast_to(slot_r, (8, TB))

    pl.semaphore_wait(barrier, len(others))

    def z_copy(d):
        return send(zx.at[z], zx.at[z], s_z.at[d], r_z.at[d], at_z(d))

    far_first = sorted(range(1, Z), key=lambda d: -min(d, Z - d))
    for d in far_first:
        z_copy(d).start()
    ask = [send(req.at[mq], req.at[mq], s_q.at[k], r_q.at[k], plane_peer(k)[0]) for k in range(1, PLANE)]
    for copy in ask:
        copy.start()
    halos = [
        send(share, win.at[pl.ds(RB + 2 * m, 2)], s_h.at[m], r_h.at[m], at_part(d))
        for m, d in enumerate(halo_steps)
    ]
    for copy in halos:
        copy.start()
    probes = [send(xy.at[y], xy.at[y], s_y.at[d], r_y.at[d], at_y(d)) for d in range(1, Y)]
    for copy in probes:
        copy.start()

    for copy in ask:
        copy.wait()
    to_req = pltpu.make_async_copy(req, req_s, loc_sem.at[2])
    to_meta = pltpu.make_async_copy(meta, meta_s, loc_sem.at[3])
    to_req.start()
    to_meta.start()

    for copy in halos:
        copy.wait()
    q_in.wait()

    def prior(r, carry):
        total = jnp.zeros((COLS, TB), F32)
        for k in range(NB):
            total += lax.dot_general(win[qc_ref[r, k]], q_v[r * NB + k], NT, preferred_element_type=F32)
        acc[r] = total
        return carry

    lax.fori_loop(0, RB, prior, 0)
    to_req.wait()
    to_meta.wait()
    a_in.wait()

    for d in far_first:
        z_copy(d).wait()

    def picked(k):
        _, q = plane_peer(k)

        def pick(s, carry):
            for j in range(2):
                sub = jnp.maximum(req_s[q, mq, 2 * s + j], 0)
                block = zx[s, sub]
                if k:
                    stage[k, 2 * s + j] = block
                else:
                    xs[mq * SLOTS + 2 * s + j] = block
            return carry

        lax.fori_loop(0, Z, pick, 0, unroll=4)

    gives = []
    for k in [6, 7, 2, 3, 4, 5, 1, 0]:
        picked(k)
        if k:
            copy = send(
                stage.at[k], xs.at[pl.ds(mq * SLOTS, SLOTS)], s_p.at[k], r_p.at[k], plane_peer(k)[0])
            copy.start()
            gives.append(copy)
    for copy in gives:
        copy.wait()

    def term(t, carry):
        tile = a_v[t]
        projected = lax.dot_general(xs[meta_s[2 * PLANE, t]], tile, NT, preferred_element_type=F32)
        weighted = (prec[pl.ds(t, 1), :] * projected).astype(BF16)
        cb[t] = lax.dot_general(weighted, tile, NN, preferred_element_type=F32)
        return carry

    lax.fori_loop(0, TILES, term, 0, unroll=8)
    cb[TILES] = jnp.zeros((COLS, TB), F32)

    backs = []
    for k in [6, 7, 2, 3, 4, 5, 1, 0]:
        where, q = plane_peer(k)

        def place(s, carry, k=k, q=q):
            block = cb[meta_s[PLANE + q, s]]
            if k:
                stage2[k, s] = block
            else:
                rc[mq, s] = block
            return carry

        lax.fori_loop(0, SLOTS, place, 0, unroll=8)
        if k:
            copy = send(stage2.at[k], rc.at[mq], s_c.at[k], r_c.at[k], where)
            copy.start()
            backs.append(copy)
    for copy in backs:
        copy.wait()

    def d_copy(d):
        return send(dn.at[d], zr.at[d], s_d.at[d], r_d.at[d], at_z(d))

    def dense(d, carry):
        dest = lax.rem(z + d, Z)
        totals = [jnp.zeros((COLS, TB), F32) for _ in range(RB)]
        for q in range(PLANE):
            for j in range(2):
                sub = jnp.broadcast_to(req_s[q, mq, 2 * dest + j], (COLS, TB))
                block = rc[q, 2 * dest + j]
                totals = [total + jnp.where(sub == r, block, 0.0) for r, total in enumerate(totals)]
        for r in range(RB):
            dn[d, r] = totals[r]
        return carry

    def dense_out(d, carry):
        dense(d, carry)
        d_copy(d).start()
        return carry

    lax.fori_loop(1, Z, dense_out, 0)
    dense(0, 0)
    for r in range(RB):
        acc[r] += dn[0, r]

    def landed(d, carry):
        d_copy(d).wait()
        for r in range(RB):
            acc[r] += zr[d, r]
        return carry

    lax.fori_loop(1, Z, landed, 0)
    for copy in probes:
        copy.wait()

    part = jnp.zeros((COLS, COLS * Y), F32)
    for r in range(RB):
        total = acc[r]
        y_ref[:, r * TB:(r + 1) * TB] = total
        across = jnp.concatenate([xy[i, :, r * TB:(r + 1) * TB] for i in range(Y)], axis=0)
        part += lax.dot_general(
            total, across.astype(F32), NT, precision=lax.Precision.HIGHEST, preferred_element_type=F32)
    gp[...] = jnp.zeros((COLS, TB), F32)
    gp[:, :COLS * Y] = part
    firsts = [send(gp, g1.at[k], s_g1.at[k], r_g1.at[k], plane_peer(k)[0]) for k in range(1, PLANE)]
    for copy in firsts:
        copy.start()
    g1[0] = gp[...]
    for copy in firsts:
        copy.wait()
    g2[0] = jnp.sum(g1[...], axis=0)
    seconds = [send(g2.at[0], g2.at[d], s_g2.at[d], r_g2.at[d], at_z(d)) for d in range(1, Z)]
    for copy in seconds:
        copy.start()
    for copy in seconds:
        copy.wait()
    g_ref[...] = jnp.sum(g2[...], axis=0) * (1.0 / math.sqrt(RB * TB * PARTS))


def body(x_cols, q_tiles, q_cols, halo_ids, a_tiles, obs_prec, tile_owner, tile_sub):
    vmem = pl.BlockSpec(memory_space=pltpu.VMEM)
    smem = pl.BlockSpec(memory_space=pltpu.SMEM)
    hbm = pl.BlockSpec(memory_space=pl.ANY)
    dma = pltpu.SemaphoreType.DMA
    block = (COLS, TB)
    product, gram = pl.pallas_call(
        kernel,
        out_shape=(
            jax.ShapeDtypeStruct((COLS, RB * TB), F32),
            jax.ShapeDtypeStruct((COLS, TB), F32),
        ),
        in_specs=[vmem, smem, smem, vmem, vmem, vmem, hbm, hbm],
        out_specs=(vmem, vmem),
        scratch_shapes=[
            pltpu.VMEM((RB * NB, TB, TB), BF16),
            pltpu.VMEM((TILES, TB, TB), BF16),
            pltpu.VMEM((RB + 8, *block), BF16),
            pltpu.VMEM((2, *block), BF16),
            pltpu.VMEM((Z, RB, *block), BF16),
            pltpu.VMEM((Y, COLS, RB * TB), BF16),
            pltpu.VMEM((PLANE, PLANE, TB), jnp.int32),
            pltpu.VMEM((2 * PLANE + 8, TB), jnp.int32),
            pltpu.SMEM((PLANE, PLANE, TB), jnp.int32),
            pltpu.SMEM((2 * PLANE + 8, TB), jnp.int32),
            pltpu.VMEM((PLANE, SLOTS, *block), BF16),
            pltpu.VMEM((PLANE * SLOTS, *block), BF16),
            pltpu.VMEM((TILES + 1, *block), F32),
            pltpu.VMEM((PLANE, SLOTS, *block), F32),
            pltpu.VMEM((PLANE, SLOTS, *block), F32),
            pltpu.VMEM((Z, RB, *block), F32),
            pltpu.VMEM((Z, RB, *block), F32),
            pltpu.VMEM((RB, *block), F32),
            pltpu.VMEM((PLANE, *block), F32),
            pltpu.VMEM((Z, *block), F32),
            pltpu.VMEM(block, F32),
            pltpu.VMEM((TILES, TB), F32),
            pltpu.VMEM((RB, *block), BF16),
            dma((4,)),
            dma((Z,)), dma((Z,)),
            dma((PLANE,)), dma((PLANE,)),
            dma((Y,)), dma((Y,)),
            dma((4,)), dma((4,)),
            dma((PLANE,)), dma((PLANE,)),
            dma((PLANE,)), dma((PLANE,)),
            dma((Z,)), dma((Z,)),
            dma((PLANE,)), dma((PLANE,)),
            dma((Z,)), dma((Z,)),
        ],
        compiler_params=pltpu.CompilerParams(
            collective_id=0, has_side_effects=True, vmem_limit_bytes=40 * 2**20),
        name="exchange",
    )(x_cols, q_cols, halo_ids, obs_prec, tile_owner, jnp.pad(tile_sub, (0, TB - TILES)).reshape(1, TB), q_tiles, a_tiles)
    return product, gram[:, :COLS * Y].T


def solution(mesh):
    torus = Mesh(mesh.devices.reshape(Z, X, C, Y), ("z", "x", "core", "col"))
    parts = ("z", "x", "core")
    in_specs = (
        P("col", parts),
        P(parts, None, None),
        P(parts, None),
        P(parts, None),
        P(parts, None, None),
        P(parts, None),
        P(parts, None),
        P(parts),
    )
    out_specs = (P("col", parts), P(None, "col"))
    return jax.shard_map(body, mesh=torus, in_specs=in_specs, out_specs=out_specs, check_vma=False)
```

time: 208 us -> 115 us (0.55)
  Pallas kernels: 0 us -> 105 us
  blocking collectives: 79.8 us -> 0 us
  waiting for transfers between devices: 59.2 us -> 0 us
  starting transfers between devices: 33 us -> 0 us
  matrix products: 17.5 us -> 0 us
  local copies, waits for them, and re-layouts: 13.3 us -> 8.29 us
  other arithmetic: 3.34 us -> 0 us
    pallas_call x0 -> x1, Pallas kernels: none -> 105 us  [body(): pl.pallas_call(kernel, out_shape=(jax.ShapeDtypeStruct((COLS, RB * TB), F...]
    psum x3 -> x0, blocking collectives: 44.7 us -> none  [over_axes(): array = lax.psum(array, axis)]
    all_to_all x1 -> x0, blocking collectives: 35.1 us -> none  [body(): lax.all_to_all(asked_ids, MESH, split_axis=0, concat_axis=0, tiled=True)]
    ppermute x4 -> x0, waiting for transfers between devices: 34 us -> none  [passed_along(): lax.ppermute(array, axis, [(i, (i + by) % length) for i in range(length)])]
    all_to_all x3 -> x0, waiting for transfers between devices: 25.2 us -> none  [the longest x1 21.3 us: body(): lax.all_to_all(answer, MESH, split_axis=0, concat_axis=0, tiled=True)]
    all_to_all x3 -> x0, starting transfers between devices: 18.6 us -> none  [the longest x1 8.78 us: body(): lax.all_to_all(sent_terms, MESH, split_axis=0, concat_axis=0, tiled=True)]
    dot_general x7 -> x0, matrix products: 17.5 us -> none  [the longest x1 13.2 us: tile_terms(): jnp.einsum('ton,tco->tcn', obs_tiles, weighted, preferred_element_type=jn...]
    ppermute x4 -> x0, starting transfers between devices: 14.3 us -> none  [passed_along(): lax.ppermute(array, axis, [(i, (i + by) % length) for i in range(length)])]
  transfers between devices with their start and end apart: 7 -> 0, of which waited for: 3 -> 0; matrix products, arithmetic and copies ran while one was open for 7% -> 0% of each run, Pallas kernels for 0% -> 0%
where the time goes in v1:
time: 115 us; the launch traced here: 114 us
  Pallas kernels  105 us (91%)
  local copies, waits for them, and re-layouts  8.29 us (7%)
    pallas_call x1, Pallas kernels, body(): pl.pallas_call(kernel, out_shape=(jax.ShapeDtypeStruct((COLS, RB * TB), F...  105 us
    unnamed x14, local copies, waits for them, and re-layouts  7.04 us

profile of v1, /device:TPU:1, one launch (start us, length us, event | category | flops | bytes accessed | tf_op | source)
XLA Modules:
  0.0 114.0 jit_solution(15306153389577045769)
XLA Ops:
  0.6 0.7 pad_bitcast_fusion.sub_ref
  1.3 0.7 copy.10.owner_ref
  2.0 0.0 copy-start
  2.0 1.6 %copy-done = bf16[64,128,128]{2,1,0:T(8,128)(2,1)S(1)} copy-done((bf16[64,128,128]{2,1,0:T(8,128)(2,1)S(1)}, bf16[64,128,128]{2,1,0:T(8,128)(2,1)}, u32[]{:S(2)}) %copy-start) | copy-done | bytes 2097176
  3.6 0.0 copy-start.1
  3.6 1.3 %copy-done.1 = bf16[40,128,128]{2,1,0:T(8,128)(2,1)S(1)} copy-done((bf16[40,128,128]{2,1,0:T(8,128)(2,1)S(1)}, bf16[40,128,128]{2,1,0:T(8,128)(2,1)}, u32[]{:S(2)}) %copy-start.1) | copy-done | bytes 1310744
  4.9 0.0 copy-start.2
  4.9 0.7 copy-done.2
  5.7 0.0 copy-start.3
  5.7 0.7 copy-done.3
  6.4 0.0 copy-start.4
  6.4 0.7 copy-done.4
  7.1 0.0 copy-start.5
  7.1 0.7 copy-done.5
  7.7 105.1 %exchange.1 = (f32[8,1024]{1,0:T(8,128)S(1)}, f32[8,128]{1,0:T(8,128)S(1)}) custom-call(bf16[8,1024]{1,0:T(8,128)(2,1)S(1)} %copy-done.2, s32[8,5]{1,0:T(8,128)S(1)} %copy-done.4, s32[1,2]{1,0:T(1,128)S(1)} %copy-done.5, bf16[64,128]{1,0:T(8,128)(2,1)S(1)} %copy-done.3, s32[64,1]{1,0:T(8,128)S(1)} %copy.10.owner_ref, s32[1,128]{1,0:T(1,128)S(1)} %pad_bitcast_fusion.sub_ref, ...), custom_call_target="tpu_custom_call" | custom-call | tf_op jit(solution)/shard_map/exchange/pallas_call | solution.py:269
  112.8 0.6 slice_bitcast_fusion
  113.4 0.6 copy.12
Async XLA Ops:
  2.0 1.6 %copy-start = (bf16[64,128,128]{2,1,0:T(8,128)(2,1)S(1)}, bf16[64,128,128]{2,1,0:T(8,128)(2,1)}, u32[]{:S(2)}) copy-start(bf16[64,128,128]{2,1,0:T(8,128)(2,1)} %a_hbm.1) | copy-start | bytes 6291460
  3.6 1.3 %copy-start.1 = (bf16[40,128,128]{2,1,0:T(8,128)(2,1)S(1)}, bf16[40,128,128]{2,1,0:T(8,128)(2,1)}, u32[]{:S(2)}) copy-start(bf16[40,128,128]{2,1,0:T(8,128)(2,1)} %q_hbm.1) | copy-start | bytes 3932164
  4.9 0.7 copy-start.2
  5.7 0.7 copy-start.3
  6.4 0.7 copy-start.4
  7.1 0.7 copy-start.5

commit v2 on v1

v2 whole, which is shorter than its diff:
```python
import math

import jax
import jax.numpy as jnp
from jax import lax
from jax.experimental import pallas as pl
from jax.experimental.pallas import tpu as pltpu
from jax.sharding import Mesh
from jax.sharding import PartitionSpec as P

LOGICAL = pl.DeviceIdType.MESH
Z, X, C, Y = 16, 4, 2, 4
PLANE = X * C
PARTS = Z * PLANE
TB = 128
COLS = 8
RB = 8
NB = 5
TILES = 64
SLOTS = 2 * Z
F32 = jnp.float32
BF16 = jnp.bfloat16
GROUP = 8
Z_PLAN = [(0, 5, None), (0, -5, None), (0, 1, None), (0, -1, None), (0, 2, None), (0, -2, None)]
Z_OWN = len(Z_PLAN)
Z_PLAN += [(-5, 3, 0), (-5, 2, None), (-5, -2, None), (-5, 1, None), (-5, -1, None)]
Z_PLAN += [(5, -3, 1), (5, 2, None), (5, -2, None), (5, 1, None), (5, -1, None)]
N_PLAN = [(8, -3, 0), (13, 2, None), (9, -2, None), (12, 1, None), (10, -1, None)]
N_PLAN += [(8, 3, 1), (7, 2, None), (3, -2, None), (6, 1, None), (4, -1, None)]
NT = (((1,), (1,)), ((), ()))
NN = (((1,), (0,)), ((), ()))


def kernel(
    x_hbm, qc_hbm, halo_hbm, prec_hbm, owner_hbm, sub_hbm, q_hbm, a_hbm,
    y_ref, g_ref,
    x_v, qc_s, halo_s, prec_in, own_v, sub_v,
    q_v, a_v, win, mine, share, zx, xy, req, meta, req_s, meta_s, stage, xs, cb, stage2, rc, dn, near, csum, direct,
    far, acc, g1, g2, gp, prec, pb, wb, pg,
    loc_sem, s_z, r_z, s_q, r_q, s_y, r_y, s_h, r_h, s_p, r_p, s_c, r_c, s_n, r_n, s_d, r_d, s_f, r_f, s_j, r_j,
    s_g1, r_g1, s_g2, r_g2,
):
    z, x, c, y = (lax.axis_index(n) for n in ("z", "x", "core", "col"))
    mq = x * C + c
    me = z * PLANE + mq

    def round_z(d):
        return lax.rem(z + d + Z, Z)

    def at_z(d):
        return {"z": round_z(d)}

    def plane_peer(k):
        px, pc = lax.rem(x + k // C, X), lax.rem(c + k % C, C)
        return {"x": px, "core": pc}, px * C + pc

    def at_part(d):
        p = lax.rem(me + d + PARTS, PARTS)
        return {"z": p // PLANE, "x": lax.rem(p // C, X), "core": lax.rem(p, C)}

    def at_y(d):
        return {"col": lax.rem(y + d, Y)}

    def send(src, dst, sems, i, where):
        return pltpu.make_async_remote_copy(
            src_ref=src, dst_ref=dst, send_sem=sems[0].at[i], recv_sem=sems[1].at[i],
            device_id=where, device_id_type=LOGICAL,
        )

    def start(copies):
        for copy in copies:
            copy.start()
        return copies

    def finish(copies):
        for copy in copies:
            copy.wait()

    loads = [
        pltpu.make_async_copy(src, dst, loc_sem.at[i])
        for i, (src, dst) in enumerate((
            (x_hbm, x_v), (halo_hbm, halo_s), (owner_hbm, own_v), (sub_hbm, sub_v), (prec_hbm, prec_in),
            (qc_hbm, qc_s), (q_hbm, q_v), (a_hbm, a_v),
        ))
    ]
    start(loads)
    x_in, halo_in, own_in, sub_in, prec_load, qc_in, q_in, a_in = loads

    barrier = pltpu.get_barrier_semaphore()
    halo_steps = (2, 1, -1, -2)
    others = [at_z(d) for d in range(1, Z)] + [plane_peer(k)[0] for k in range(1, PLANE)]
    others += [at_part(d) for d in halo_steps] + [at_y(d) for d in range(1, Y)]
    for other in others:
        pl.semaphore_signal(barrier, inc=1, device_id=other, device_id_type=LOGICAL)

    x_in.wait()
    halo_in.wait()
    for r in range(RB):
        block = x_v[:, r * TB:(r + 1) * TB]
        win[r] = block
        mine[r] = block
        zx[z, r] = block
    xy[y] = x_v[...]
    for h in range(2):
        share[h] = mine[halo_s[0, h]]

    def z_copy(i):
        hold, step, half = Z_PLAN[i]
        origin = round_z(hold)
        part = zx.at[origin] if half is None else zx.at[origin, pl.ds(half * (RB // 2), RB // 2)]
        return send(part, part, (s_z, r_z), i, at_z(step))

    z_copies = [z_copy(i) for i in range(len(Z_PLAN))]

    pl.semaphore_wait(barrier, len(others))

    start(z_copies[:Z_OWN])
    halos = start([
        send(share, win.at[pl.ds(RB + 2 * m, 2)], (s_h, r_h), m, at_part(d))
        for m, d in enumerate(halo_steps)
    ])
    probes = start([send(x_v, xy.at[y], (s_y, r_y), d, at_y(d)) for d in range(1, Y)])

    own_in.wait()
    sub_in.wait()
    prec_load.wait()
    prec[...] = prec_in[...].astype(F32)
    shape = (TILES, TB)
    lane = lax.broadcasted_iota(jnp.int32, shape, 1)
    row = lax.broadcasted_iota(jnp.int32, shape, 0)
    eye = lane == row
    fill = jnp.full((1, TB - TILES), -1, jnp.int32)
    own_r = jnp.concatenate([own_v[...], fill], axis=1)
    sub_r = jnp.concatenate([sub_v[...], fill], axis=1)
    own_b = jnp.broadcast_to(jnp.sum(jnp.where(eye, own_r, 0), axis=1, keepdims=True), shape)
    sub_b = jnp.broadcast_to(jnp.sum(jnp.where(eye, sub_r, 0), axis=1, keepdims=True), shape)
    same = own_b == own_r
    j_b = jnp.broadcast_to(
        jnp.sum(jnp.where(same & (lane < row), 1, 0), axis=1, keepdims=True), shape)
    j_r = jnp.sum(jnp.where(same & (row < lane), 1, 0), axis=0, keepdims=True)
    col_b = jnp.bitwise_and(own_b, PLANE - 1)
    key_b = jnp.right_shift(own_b, 3) * 2 + j_b
    for q in range(PLANE):
        hit = (col_b == q) & (key_b == lane)
        wanted = jnp.sum(jnp.where(hit, sub_b + 1, 0), axis=0, keepdims=True) - 1
        req[mq, q:q + 1] = wanted
        meta[PLANE + q:PLANE + q + 1] = jnp.sum(jnp.where(hit, row - TILES, 0), axis=0, keepdims=True) + TILES
    slot_r = jnp.bitwise_and(own_r, PLANE - 1) * SLOTS + jnp.right_shift(own_r, 3) * 2 + j_r
    meta[:PLANE] = jnp.broadcast_to(slot_r, (8, TB))
    to_meta = pltpu.make_async_copy(meta, meta_s, loc_sem.at[8])
    to_meta.start()
    asks = start([send(req.at[mq], req.at[mq], (s_q, r_q), k, plane_peer(k)[0]) for k in range(1, PLANE)])

    for i in range(2):
        z_copies[i].wait_recv()
        start(z_copies[Z_OWN + 5 * i:Z_OWN + 5 * i + 5])

    finish(asks)
    to_req = pltpu.make_async_copy(req, req_s, loc_sem.at[9])
    to_req.start()

    finish(halos)
    qc_in.wait()
    q_in.wait()

    def prior(r, carry):
        total = jnp.zeros((COLS, TB), F32)
        for k in range(NB):
            total += lax.dot_general(win[qc_s[r, k]], q_v[r * NB + k], NT, preferred_element_type=F32)
        acc[r] = total
        return carry

    lax.fori_loop(0, RB, prior, 0, unroll=2)
    to_req.wait()
    to_meta.wait()
    a_in.wait()

    for i, copy in enumerate(z_copies):
        copy.wait_send()
        if i >= 2:
            copy.wait_recv()

    order = [6, 7, 2, 3, 4, 5, 1, 0]
    gives = []
    for k in order:
        where, q = plane_peer(k)

        def pick(s, carry, k=k, q=q):
            for j in range(2):
                block = zx[s, jnp.maximum(req_s[q, mq, 2 * s + j], 0)]
                if k:
                    stage[k, 2 * s + j] = block
                else:
                    xs[mq * SLOTS + 2 * s + j] = block
            return carry

        lax.fori_loop(0, Z, pick, 0, unroll=8)
        if k:
            gives += start([send(stage.at[k], xs.at[pl.ds(mq * SLOTS, SLOTS)], (s_p, r_p), k, where)])
    finish(gives)

    def terms(group, carry):
        base = pl.multiple_of(group * GROUP, GROUP)
        scales = prec[pl.ds(base, GROUP), :]
        tiles, projected, weighted = [], [], []
        for i in range(0, GROUP, 2):
            tile = a_v[pl.ds(base + i, 2)].reshape(2 * TB, TB)
            pair = jnp.concatenate([xs[meta_s[0, base + i]], xs[meta_s[0, base + i + 1]]], axis=0)
            tiles.append(tile)
            projected.append(lax.dot_general(pair, tile, NT, preferred_element_type=F32))
        zero = jnp.zeros((COLS, TB), F32)
        for i in range(0, GROUP, 2):
            both = projected[i // 2]
            top, low = both[:COLS, :TB], both[COLS:, TB:]
            top_w, low_w = scales[i:i + 1] * top, scales[i + 1:i + 2] * low
            block = jnp.concatenate([
                jnp.concatenate([top_w, zero], axis=1), jnp.concatenate([zero, low_w], axis=1)], axis=0)
            weighted.append(block.astype(BF16))
            for h, (p, w) in enumerate(((top, top_w), (low, low_w))):
                lanes = pl.ds(pl.multiple_of((base + i + h) * TB, TB), TB)
                pb[:, lanes] = p.astype(BF16)
                wb[:, lanes] = w.astype(BF16)
        for i in range(0, GROUP, 2):
            both = lax.dot_general(weighted[i // 2], tiles[i // 2], NN, preferred_element_type=F32)
            cb[base + i] = both[:COLS]
            cb[base + i + 1] = both[COLS:]
        return carry

    lax.fori_loop(0, TILES // GROUP, terms, 0)
    cb[TILES] = jnp.zeros((COLS, TB), F32)

    backs = []
    for k in order:
        where, q = plane_peer(k)

        def place(s, carry, k=k, q=q):
            block = cb[meta_s[PLANE + q, s]]
            if k:
                stage2[k, s] = block
            else:
                rc[mq, s] = block
            return carry

        lax.fori_loop(0, SLOTS, place, 0, unroll=8)
        if k:
            backs += start([send(stage2.at[k], rc.at[mq], (s_c, r_c), k, where)])

    turns = start([send(pb, pg.at[y], (s_j, r_j), d, at_y(d)) for d in range(1, Y)])
    pg[y] = pb[...]
    finish(probes)
    part = jnp.zeros((COLS, COLS * Y), F32)
    for r in range(RB):
        across = jnp.concatenate([xy[i, :, r * TB:(r + 1) * TB] for i in range(Y)], axis=0)
        part += lax.dot_general(
            acc[r], across.astype(F32), NT, precision=lax.Precision.HIGHEST, preferred_element_type=F32)
    finish(turns)

    def gram_part(i, part):
        lanes = pl.ds(pl.multiple_of(i * 1024, 1024), 1024)
        across = jnp.concatenate([pg[j, :, lanes] for j in range(Y)], axis=0)
        return part + lax.dot_general(wb[:, lanes], across, NT, preferred_element_type=F32)

    part = lax.fori_loop(0, TILES * TB // 1024, gram_part, part)
    gp[...] = jnp.zeros((COLS, TB), F32)
    gp[:, :COLS * Y] = part
    firsts = start([send(gp, g1.at[k], (s_g1, r_g1), k, plane_peer(k)[0]) for k in range(1, PLANE)])
    g1[0] = gp[...]
    finish(backs)

    def dense(i, carry):
        d = lax.rem(i, Z)
        dest = lax.rem(z + d, Z)
        totals = [jnp.zeros((COLS, TB), F32) for _ in range(RB)]
        for q in range(PLANE):
            for j in range(2):
                sub = jnp.broadcast_to(req_s[q, mq, 2 * dest + j], (COLS, TB))
                block = rc[q, 2 * dest + j]
                totals = [total + jnp.where(sub == r, block, 0.0) for r, total in enumerate(totals)]
        for r in range(RB):
            dn[d, r] = totals[r]
        return carry

    lax.fori_loop(3, 14, dense, 0)
    nears = []
    for i, (d, step, half) in enumerate(N_PLAN):
        if half is None:
            src, dst = dn.at[d], near.at[i]
        else:
            rows = pl.ds(half * (RB // 2), RB // 2)
            src, dst = dn.at[d, rows], near.at[i, rows]
        nears += start([send(src, dst, (s_n, r_n), i, at_z(step))])
    lax.fori_loop(14, 19, dense, 0)
    directs = start([send(dn.at[d % Z], direct.at[i], (s_d, r_d), i, at_z(d)) for i, d in enumerate((1, -1, 2, -2))])
    finish(firsts)
    g2[0] = jnp.sum(g1[...], axis=0)
    seconds = start([send(g2.at[0], g2.at[d], (s_g2, r_g2), d, at_z(d)) for d in range(1, Z)])

    finish(nears)
    fars = []
    for g, d in enumerate((-5, 5)):
        for r in range(RB):
            total = dn[d % Z, r]
            for i in range(4):
                total += near[5 * g + 1 + i, r]
            if r // (RB // 2) == g:
                total += near[5 * g, r]
            csum[g, r] = total
        fars += start([send(csum.at[g], far.at[g], (s_f, r_f), g, at_z(d))])
    finish(directs)
    for r in range(RB):
        acc[r] += (dn[0, r] + direct[0, r]) + (direct[1, r] + direct[2, r]) + direct[3, r]
    finish(seconds)
    g_ref[...] = (jnp.sum(g2[...], axis=0) * (1.0 / math.sqrt(RB * TB * PARTS)))[:, :COLS * Y]
    finish(fars)
    for r in range(RB):
        y_ref[:, r * TB:(r + 1) * TB] = acc[r] + (far[0, r] + far[1, r])


def body(x_cols, q_tiles, q_cols, halo_ids, a_tiles, obs_prec, tile_owner, tile_sub):
    vmem = pl.BlockSpec(memory_space=pltpu.VMEM)
    hbm = pl.BlockSpec(memory_space=pl.ANY)
    block = (COLS, TB)

    def pair(n):
        return [pltpu.SemaphoreType.DMA((n,))] * 2

    product, gram = pl.pallas_call(
        kernel,
        out_shape=(
            jax.ShapeDtypeStruct((COLS, RB * TB), F32),
            jax.ShapeDtypeStruct((COLS, COLS * Y), F32),
        ),
        in_specs=[hbm] * 8,
        out_specs=(vmem, vmem),
        scratch_shapes=[
            pltpu.VMEM((COLS, RB * TB), BF16),
            pltpu.SMEM((RB, NB), jnp.int32),
            pltpu.SMEM((1, 2), jnp.int32),
            pltpu.VMEM((TILES, TB), BF16),
            pltpu.VMEM((1, TILES), jnp.int32),
            pltpu.VMEM((1, TILES), jnp.int32),
            pltpu.VMEM((RB * NB, TB, TB), BF16),
            pltpu.VMEM((TILES, TB, TB), BF16),
            pltpu.VMEM((RB + 8, *block), BF16),
            pltpu.VMEM((RB, *block), BF16),
            pltpu.VMEM((2, *block), BF16),
            pltpu.VMEM((Z, RB, *block), BF16),
            pltpu.VMEM((Y, COLS, RB * TB), BF16),
            pltpu.VMEM((PLANE, PLANE, TB), jnp.int32),
            pltpu.VMEM((2 * PLANE, TB), jnp.int32),
            pltpu.SMEM((PLANE, PLANE, TB), jnp.int32),
            pltpu.SMEM((2 * PLANE, TB), jnp.int32),
            pltpu.VMEM((PLANE, SLOTS, *block), BF16),
            pltpu.VMEM((PLANE * SLOTS, *block), BF16),
            pltpu.VMEM((TILES + 1, *block), F32),
            pltpu.VMEM((PLANE, SLOTS, *block), F32),
            pltpu.VMEM((PLANE, SLOTS, *block), F32),
            pltpu.VMEM((Z, RB, *block), F32),
            pltpu.VMEM((len(N_PLAN), RB, *block), F32),
            pltpu.VMEM((2, RB, *block), F32),
            pltpu.VMEM((4, RB, *block), F32),
            pltpu.VMEM((2, RB, *block), F32),
            pltpu.VMEM((RB, *block), F32),
            pltpu.VMEM((PLANE, *block), F32),
            pltpu.VMEM((Z, *block), F32),
            pltpu.VMEM(block, F32),
            pltpu.VMEM((TILES, TB), F32),
            pltpu.VMEM((COLS, TILES * TB), BF16),
            pltpu.VMEM((COLS, TILES * TB), BF16),
            pltpu.VMEM((Y, COLS, TILES * TB), BF16),
            pltpu.SemaphoreType.DMA((10,)),
            *pair(len(Z_PLAN)),
            *pair(PLANE),
            *pair(Y),
            *pair(4),
            *pair(PLANE),
            *pair(PLANE),
            *pair(len(N_PLAN)),
            *pair(4),
            *pair(2),
            *pair(Y),
            *pair(PLANE),
            *pair(Z),
        ],
        compiler_params=pltpu.CompilerParams(
            collective_id=0, has_side_effects=True, vmem_limit_bytes=60 * 2**20),
        name="exchange",
    )(
        x_cols, q_cols, halo_ids, obs_prec, tile_owner.reshape(1, TILES), tile_sub.reshape(1, TILES),
        q_tiles, a_tiles,
    )
    return product, gram.T


def solution(mesh):
    torus = Mesh(mesh.devices.reshape(Z, X, C, Y), ("z", "x", "core", "col"))
    parts = ("z", "x", "core")
    in_specs = (
        P("col", parts),
        P(parts, None, None),
        P(parts, None),
        P(parts, None),
        P(parts, None, None),
        P(parts, None),
        P(parts, None),
        P(parts),
    )
    out_specs = (P("col", parts), P(None, "col"))
    return jax.shard_map(body, mesh=torus, in_specs=in_specs, out_specs=out_specs, check_vma=False)
```

time: 115 us -> 73.4 us (0.64)
  Pallas kernels: 105 us -> 69.9 us
  local copies, waits for them, and re-layouts: 8.29 us -> 2.65 us
    pallas_call x1, Pallas kernels: 105 us -> 69.9 us  [body(): pl.pallas_call(kernel, out_shape=(jax.ShapeDtypeStruct((COLS, RB * TB), F...]
    unnamed x14 -> x2, local copies, waits for them, and re-layouts: 7.04 us -> 2.65 us
where the time goes in v2:
time: 73.4 us; the launch traced here: 73.2 us
  Pallas kernels  69.9 us (95%)
  local copies, waits for them, and re-layouts  2.65 us (4%)
    pallas_call x1, Pallas kernels, body(): pl.pallas_call(kernel, out_shape=(jax.ShapeDtypeStruct((COLS, RB * TB), F...  69.9 us
    unnamed x2, local copies, waits for them, and re-layouts  2.65 us

profile of v2, /device:TPU:1, one launch (start us, length us, event | category | flops | bytes accessed | tf_op | source)
XLA Modules:
  0.0 73.2 jit_solution(551052325436764681)
XLA Ops:
  0.6 69.9 %exchange.1 = (f32[8,1024]{1,0:T(8,128)}, f32[8,32]{1,0:T(8,128)}) custom-call(bf16[8,1024]{1,0:T(8,128)(2,1)} %x_hbm.1, s32[8,5]{1,0:T(8,128)} %qc_hbm.1, s32[1,2]{1,0:T(1,128)} %halo_hbm.1, bf16[64,128]{1,0:T(8,128)(2,1)} %prec_hbm.1, s32[1,64]{1,0:T(1,128)} %bitcast.4, s32[1,64]{1,0:T(1,128)} %bitcast.5, bf16[40,128,128]{2,1,0:T(8,128)(2,1)} %q_hbm.1, ...), custom_call_target="tpu_custom_call" | custom-call | tf_op jit(solution)/shard_map/exchange/pallas_call | solution.py:327
  70.5 1.4 %copy.12 = f32[8,1024]{1,0:T(8,128)} copy(f32[8,1024]{1,0:T(8,128)} %get-tuple-element.8) | data formatting | bytes 65536
  71.9 1.3 %copy.13 = f32[32,8]{0,1:T(8,128)} copy(f32[32,8]{0,1:T(8,128)} %bitcast.3) | data formatting | bytes 2048

commit v3 on v2

--- a/solution.py
+++ b/solution.py
@@ -25,6 +25,9 @@
 Z_OWN = len(Z_PLAN)
 Z_PLAN += [(-5, 3, 0), (-5, 2, None), (-5, -2, None), (-5, 1, None), (-5, -1, None)]
 Z_PLAN += [(5, -3, 1), (5, 2, None), (5, -2, None), (5, 1, None), (5, -1, None)]
+ORDER = (0, 1, 15, 2, 14, 5, 11, 3, 4, 6, 7, 8, 9, 10, 12, 13)
+FIRST = 7
+WAVES = ((0, FIRST), (FIRST, Z))
 N_PLAN = [(8, -3, 0), (13, 2, None), (9, -2, None), (12, 1, None), (10, -1, None)]
 N_PLAN += [(8, 3, 1), (7, 2, None), (3, -2, None), (6, 1, None), (4, -1, None)]
 NT = (((1,), (1,)), ((), ()))
@@ -35,7 +38,7 @@
     x_hbm, qc_hbm, halo_hbm, prec_hbm, owner_hbm, sub_hbm, q_hbm, a_hbm,
     y_ref, g_ref,
     x_v, qc_s, halo_s, prec_in, own_v, sub_v,
-    q_v, a_v, win, mine, share, zx, xy, req, meta, req_s, meta_s, stage, xs, cb, stage2, rc, dn, near, csum, direct,
+    q_v, a_v, win, mine, share, zx, zy, xy, req, meta, req_s, meta_s, stage, xs, cb, stage2, rc, dn, near, csum, direct,
     far, acc, g1, g2, gp, prec, pb, wb, pg,
     loc_sem, s_z, r_z, s_q, r_q, s_y, r_y, s_h, r_h, s_p, r_p, s_c, r_c, s_n, r_n, s_d, r_d, s_f, r_f, s_j, r_j,
     s_g1, r_g1, s_g2, r_g2,
@@ -99,16 +102,22 @@
         block = x_v[:, r * TB:(r + 1) * TB]
         win[r] = block
         mine[r] = block
-        zx[z, r] = block
+        zx[0, r] = block
     xy[y] = x_v[...]
     for h in range(2):
         share[h] = mine[halo_s[0, h]]
 
+    def chunk(d):
+        i = ORDER.index(d % Z)
+        return zx.at[i] if i < FIRST else zy.at[i - FIRST]
+
     def z_copy(i):
         hold, step, half = Z_PLAN[i]
-        origin = round_z(hold)
-        part = zx.at[origin] if half is None else zx.at[origin, pl.ds(half * (RB // 2), RB // 2)]
-        return send(part, part, (s_z, r_z), i, at_z(step))
+        src, dst = chunk(hold), chunk(hold - step)
+        if half is not None:
+            rows = pl.ds(half * (RB // 2), RB // 2)
+            src, dst = src.at[rows], dst.at[rows]
+        return send(src, dst, (s_z, r_z), i, at_z(step))
 
     z_copies = [z_copy(i) for i in range(len(Z_PLAN))]
 
@@ -139,13 +148,18 @@
         jnp.sum(jnp.where(same & (lane < row), 1, 0), axis=1, keepdims=True), shape)
     j_r = jnp.sum(jnp.where(same & (row < lane), 1, 0), axis=0, keepdims=True)
     col_b = jnp.bitwise_and(own_b, PLANE - 1)
-    key_b = jnp.right_shift(own_b, 3) * 2 + j_b
+
+    def place_of(owner):
+        offset = jnp.bitwise_and(jnp.right_shift(owner, 3) - z, Z - 1)
+        return sum(jnp.where(offset == d, 2 * i, 0) for i, d in enumerate(ORDER) if i)
+
+    key_b = place_of(own_b) + j_b
     for q in range(PLANE):
         hit = (col_b == q) & (key_b == lane)
         wanted = jnp.sum(jnp.where(hit, sub_b + 1, 0), axis=0, keepdims=True) - 1
         req[mq, q:q + 1] = wanted
         meta[PLANE + q:PLANE + q + 1] = jnp.sum(jnp.where(hit, row - TILES, 0), axis=0, keepdims=True) + TILES
-    slot_r = jnp.bitwise_and(own_r, PLANE - 1) * SLOTS + jnp.right_shift(own_r, 3) * 2 + j_r
+    slot_r = jnp.bitwise_and(own_r, PLANE - 1) * SLOTS + place_of(own_r) + j_r
     meta[:PLANE] = jnp.broadcast_to(slot_r, (8, TB))
     to_meta = pltpu.make_async_copy(meta, meta_s, loc_sem.at[8])
     to_meta.start()
@@ -158,46 +172,43 @@
     finish(asks)
     to_req = pltpu.make_async_copy(req, req_s, loc_sem.at[9])
     to_req.start()
-
-    finish(halos)
-    qc_in.wait()
-    q_in.wait()
-
-    def prior(r, carry):
-        total = jnp.zeros((COLS, TB), F32)
-        for k in range(NB):
-            total += lax.dot_general(win[qc_s[r, k]], q_v[r * NB + k], NT, preferred_element_type=F32)
-        acc[r] = total
-        return carry
-
-    lax.fori_loop(0, RB, prior, 0, unroll=2)
+    for copy in z_copies[2:Z_OWN]:
+        copy.wait_recv()
     to_req.wait()
+
+    def give(wave, k):
+        low, high = WAVES[wave]
+        slots = pl.ds(2 * low, 2 * (high - low))
+        return send(stage.at[k, slots], xs.at[mq, slots], (s_p.at[wave], r_p.at[wave]), k, plane_peer(k)[0])
+
+    def pick(wave, k, dst):
+        _, q = plane_peer(k)
+        held, low = (zy, FIRST) if wave else (zx, 0)
+        for i in range(*WAVES[wave]):
+            for j in range(2):
+                dst[2 * i + j] = held[i - low, jnp.maximum(req_s[q, mq, 2 * i + j], 0)]
+
+    for wave in range(2):
+        if wave:
+            for copy in z_copies[Z_OWN:]:
+                copy.wait_recv()
+
+        def hand_out(i, carry, wave=wave):
+            k = lax.rem(i + 3, PLANE - 1) + 1
+            pick(wave, k, stage.at[k])
+            give(wave, k).start()
+            return carry
+
+        lax.fori_loop(0, PLANE - 1, hand_out, 0)
+        pick(wave, 0, xs.at[mq])
     to_meta.wait()
     a_in.wait()
-
-    for i, copy in enumerate(z_copies):
+    for copy in z_copies:
         copy.wait_send()
-        if i >= 2:
-            copy.wait_recv()
-
-    order = [6, 7, 2, 3, 4, 5, 1, 0]
-    gives = []
-    for k in order:
-        where, q = plane_peer(k)
-
-        def pick(s, carry, k=k, q=q):
-            for j in range(2):
-                block = zx[s, jnp.maximum(req_s[q, mq, 2 * s + j], 0)]
-                if k:
-                    stage[k, 2 * s + j] = block
-                else:
-                    xs[mq * SLOTS + 2 * s + j] = block
-            return carry
-
-        lax.fori_loop(0, Z, pick, 0, unroll=8)
-        if k:
-            gives += start([send(stage.at[k], xs.at[pl.ds(mq * SLOTS, SLOTS)], (s_p, r_p), k, where)])
-    finish(gives)
+    for wave in range(2):
+        finish([give(wave, k) for k in range(1, PLANE)])
+
+    xs_flat = xs.reshape(PLANE * SLOTS, COLS, TB)
 
     def terms(group, carry):
         base = pl.multiple_of(group * GROUP, GROUP)
@@ -205,7 +216,7 @@
         tiles, projected, weighted = [], [], []
         for i in range(0, GROUP, 2):
             tile = a_v[pl.ds(base + i, 2)].reshape(2 * TB, TB)
-            pair = jnp.concatenate([xs[meta_s[0, base + i]], xs[meta_s[0, base + i + 1]]], axis=0)
+            pair = jnp.concatenate([xs_flat[meta_s[0, base + i]], xs_flat[meta_s[0, base + i + 1]]], axis=0)
             tiles.append(tile)
             projected.append(lax.dot_general(pair, tile, NT, preferred_element_type=F32))
         zero = jnp.zeros((COLS, TB), F32)
@@ -228,25 +239,42 @@
 
     lax.fori_loop(0, TILES // GROUP, terms, 0)
     cb[TILES] = jnp.zeros((COLS, TB), F32)
-
-    backs = []
-    for k in order:
-        where, q = plane_peer(k)
-
-        def place(s, carry, k=k, q=q):
-            block = cb[meta_s[PLANE + q, s]]
-            if k:
-                stage2[k, s] = block
-            else:
-                rc[mq, s] = block
+    turns = start([send(pb, pg.at[y], (s_j, r_j), d, at_y(d)) for d in range(1, Y)])
+
+    def back(wave, k):
+        low, high = WAVES[wave]
+        slots = pl.ds(2 * low, 2 * (high - low))
+        return send(stage2.at[k, slots], rc.at[mq, slots], (s_c.at[wave], r_c.at[wave]), k, plane_peer(k)[0])
+
+    def place(wave, k, dst):
+        _, q = plane_peer(k)
+        for i in range(2 * WAVES[wave][0], 2 * WAVES[wave][1]):
+            dst[i] = cb[meta_s[PLANE + q, i]]
+
+    for wave in (1, 0):
+
+        def hand_back(i, carry, wave=wave):
+            k = lax.rem(i + 3, PLANE - 1) + 1
+            place(wave, k, stage2.at[k])
+            back(wave, k).start()
             return carry
 
-        lax.fori_loop(0, SLOTS, place, 0, unroll=8)
-        if k:
-            backs += start([send(stage2.at[k], rc.at[mq], (s_c, r_c), k, where)])
-
-    turns = start([send(pb, pg.at[y], (s_j, r_j), d, at_y(d)) for d in range(1, Y)])
+        lax.fori_loop(0, PLANE - 1, hand_back, 0)
+        place(wave, 0, rc.at[mq])
+
     pg[y] = pb[...]
+    finish(halos)
+    qc_in.wait()
+    q_in.wait()
+
+    def prior(r, carry):
+        total = jnp.zeros((COLS, TB), F32)
+        for k in range(NB):
+            total += lax.dot_general(win[qc_s[r, k]], q_v[r * NB + k], NT, preferred_element_type=F32)
+        acc[r] = total
+        return carry
+
+    lax.fori_loop(0, RB, prior, 0, unroll=4)
     finish(probes)
     part = jnp.zeros((COLS, COLS * Y), F32)
     for r in range(RB):
@@ -261,45 +289,44 @@
         return part + lax.dot_general(wb[:, lanes], across, NT, preferred_element_type=F32)
 
     part = lax.fori_loop(0, TILES * TB // 1024, gram_part, part)
-    gp[...] = jnp.zeros((COLS, TB), F32)
-    gp[:, :COLS * Y] = part
+    gp[...] = jnp.concatenate([part[2 * i:2 * i + 2] for i in range(COLS // 2)], axis=1)
     firsts = start([send(gp, g1.at[k], (s_g1, r_g1), k, plane_peer(k)[0]) for k in range(1, PLANE)])
     g1[0] = gp[...]
-    finish(backs)
 
     def dense(i, carry):
-        d = lax.rem(i, Z)
-        dest = lax.rem(z + d, Z)
         totals = [jnp.zeros((COLS, TB), F32) for _ in range(RB)]
         for q in range(PLANE):
             for j in range(2):
-                sub = jnp.broadcast_to(req_s[q, mq, 2 * dest + j], (COLS, TB))
-                block = rc[q, 2 * dest + j]
+                sub = jnp.broadcast_to(req_s[q, mq, 2 * i + j], (COLS, TB))
+                block = rc[q, 2 * i + j]
                 totals = [total + jnp.where(sub == r, block, 0.0) for r, total in enumerate(totals)]
         for r in range(RB):
-            dn[d, r] = totals[r]
+            dn[i, r] = totals[r]
         return carry
 
-    lax.fori_loop(3, 14, dense, 0)
+    def sums_for(d):
+        return dn.at[ORDER.index(d % Z)]
+
+    finish([back(1, k) for k in range(1, PLANE)])
+    lax.fori_loop(*WAVES[1], dense, 0)
     nears = []
     for i, (d, step, half) in enumerate(N_PLAN):
-        if half is None:
-            src, dst = dn.at[d], near.at[i]
-        else:
+        src, dst = sums_for(d), near.at[i]
+        if half is not None:
             rows = pl.ds(half * (RB // 2), RB // 2)
-            src, dst = dn.at[d, rows], near.at[i, rows]
+            src, dst = src.at[rows], dst.at[rows]
         nears += start([send(src, dst, (s_n, r_n), i, at_z(step))])
-    lax.fori_loop(14, 19, dense, 0)
-    directs = start([send(dn.at[d % Z], direct.at[i], (s_d, r_d), i, at_z(d)) for i, d in enumerate((1, -1, 2, -2))])
     finish(firsts)
     g2[0] = jnp.sum(g1[...], axis=0)
     seconds = start([send(g2.at[0], g2.at[d], (s_g2, r_g2), d, at_z(d)) for d in range(1, Z)])
-
+    finish([back(0, k) for k in range(1, PLANE)])
+    lax.fori_loop(*WAVES[0], dense, 0)
+    directs = start([send(sums_for(d), direct.at[i], (s_d, r_d), i, at_z(d)) for i, d in enumerate((1, -1, 2, -2))])
     finish(nears)
     fars = []
     for g, d in enumerate((-5, 5)):
         for r in range(RB):
-            total = dn[d % Z, r]
+            total = sums_for(d)[r]
             for i in range(4):
                 total += near[5 * g + 1 + i, r]
             if r // (RB // 2) == g:
@@ -310,7 +337,9 @@
     for r in range(RB):
         acc[r] += (dn[0, r] + direct[0, r]) + (direct[1, r] + direct[2, r]) + direct[3, r]
     finish(seconds)
-    g_ref[...] = (jnp.sum(g2[...], axis=0) * (1.0 / math.sqrt(RB * TB * PARTS)))[:, :COLS * Y]
+    total = jnp.sum(g2[...], axis=0) * (1.0 / math.sqrt(RB * TB * PARTS))
+    width = COLS * Y
+    g_ref[...] = jnp.concatenate([total[:, i * width:(i + 1) * width] for i in range(COLS // 2)], axis=0)
     finish(fars)
     for r in range(RB):
         y_ref[:, r * TB:(r + 1) * TB] = acc[r] + (far[0, r] + far[1, r])
@@ -321,8 +350,8 @@
     hbm = pl.BlockSpec(memory_space=pl.ANY)
     block = (COLS, TB)
 
-    def pair(n):
-        return [pltpu.SemaphoreType.DMA((n,))] * 2
+    def pair(*shape):
+        return [pltpu.SemaphoreType.DMA(shape)] * 2
 
     product, gram = pl.pallas_call(
         kernel,
@@ -344,14 +373,15 @@
             pltpu.VMEM((RB + 8, *block), BF16),
             pltpu.VMEM((RB, *block), BF16),
             pltpu.VMEM((2, *block), BF16),
-            pltpu.VMEM((Z, RB, *block), BF16),
+            pltpu.VMEM((FIRST, RB, *block), BF16),
+            pltpu.VMEM((Z - FIRST, RB, *block), BF16),
             pltpu.VMEM((Y, COLS, RB * TB), BF16),
             pltpu.VMEM((PLANE, PLANE, TB), jnp.int32),
             pltpu.VMEM((2 * PLANE, TB), jnp.int32),
             pltpu.SMEM((PLANE, PLANE, TB), jnp.int32),
             pltpu.SMEM((2 * PLANE, TB), jnp.int32),
             pltpu.VMEM((PLANE, SLOTS, *block), BF16),
-            pltpu.VMEM((PLANE * SLOTS, *block), BF16),
+            pltpu.VMEM((PLANE, SLOTS, *block), BF16),
             pltpu.VMEM((TILES + 1, *block), F32),
             pltpu.VMEM((PLANE, SLOTS, *block), F32),
             pltpu.VMEM((PLANE, SLOTS, *block), F32),
@@ -361,9 +391,9 @@
             pltpu.VMEM((4, RB, *block), F32),
             pltpu.VMEM((2, RB, *block), F32),
             pltpu.VMEM((RB, *block), F32),
-            pltpu.VMEM((PLANE, *block), F32),
-            pltpu.VMEM((Z, *block), F32),
-            pltpu.VMEM(block, F32),
+            pltpu.VMEM((PLANE, 2, TB), F32),
+            pltpu.VMEM((Z, 2, TB), F32),
+            pltpu.VMEM((2, TB), F32),
             pltpu.VMEM((TILES, TB), F32),
             pltpu.VMEM((COLS, TILES * TB), BF16),
             pltpu.VMEM((COLS, TILES * TB), BF16),
@@ -373,8 +403,8 @@
             *pair(PLANE),
             *pair(Y),
             *pair(4),
-            *pair(PLANE),
-            *pair(PLANE),
+            *pair(2, PLANE),
+            *pair(2, PLANE),
             *pair(len(N_PLAN)),
             *pair(4),
             *pair(2),

time: 73.4 us -> 65.3 us (0.89)
  Pallas kernels: 69.9 us -> 61.8 us
    pallas_call x1, Pallas kernels: 69.9 us -> 61.8 us  [body(): pl.pallas_call(kernel, out_shape=(jax.ShapeDtypeStruct((COLS, RB * TB), F...]
where the time goes in v3:
time: 65.3 us; the launch traced here: 65.1 us
  Pallas kernels  61.8 us (95%)
  local copies, waits for them, and re-layouts  2.65 us (4%)
    pallas_call x1, Pallas kernels, body(): pl.pallas_call(kernel, out_shape=(jax.ShapeDtypeStruct((COLS, RB * TB), F...  61.8 us
    unnamed x2, local copies, waits for them, and re-layouts  2.65 us

profile of v3, /device:TPU:1, one launch (start us, length us, event | category | flops | bytes accessed | tf_op | source)
XLA Modules:
  0.0 65.1 jit_solution(3441956362193939484)
XLA Ops:
  0.6 61.8 %exchange.1 = (f32[8,1024]{1,0:T(8,128)}, f32[8,32]{1,0:T(8,128)}) custom-call(bf16[8,1024]{1,0:T(8,128)(2,1)} %x_hbm.1, s32[8,5]{1,0:T(8,128)} %qc_hbm.1, s32[1,2]{1,0:T(1,128)} %halo_hbm.1, bf16[64,128]{1,0:T(8,128)(2,1)} %prec_hbm.1, s32[1,64]{1,0:T(1,128)} %bitcast.4, s32[1,64]{1,0:T(1,128)} %bitcast.5, bf16[40,128,128]{2,1,0:T(8,128)(2,1)} %q_hbm.1, ...), custom_call_target="tpu_custom_call" | custom-call | tf_op jit(solution)/shard_map/exchange/pallas_call | solution.py:356
  62.4 1.4 %copy.12 = f32[8,1024]{1,0:T(8,128)} copy(f32[8,1024]{1,0:T(8,128)} %get-tuple-element.8) | data formatting | bytes 65536
  63.8 1.3 %copy.13 = f32[32,8]{0,1:T(8,128)} copy(f32[32,8]{0,1:T(8,128)} %bitcast.3) | data formatting | bytes 2048

commit v4 on v3

--- a/solution.py
+++ b/solution.py
@@ -343,6 +343,11 @@
     finish(fars)
     for r in range(RB):
         y_ref[:, r * TB:(r + 1) * TB] = acc[r] + (far[0, r] + far[1, r])
+
+
+def settle(product_ref, gram_ref, y_ref, g_ref):
+    y_ref[...] = product_ref[...]
+    g_ref[...] = gram_ref[...]
 
 
 def body(x_cols, q_tiles, q_cols, halo_ids, a_tiles, obs_prec, tile_owner, tile_sub):
@@ -419,6 +424,11 @@
         x_cols, q_cols, halo_ids, obs_prec, tile_owner.reshape(1, TILES), tile_sub.reshape(1, TILES),
         q_tiles, a_tiles,
     )
+    product, gram = pl.pallas_call(
+        settle,
+        out_shape=(jax.ShapeDtypeStruct(product.shape, F32), jax.ShapeDtypeStruct(gram.shape, F32)),
+        name="settle",
+    )(product, gram)
     return product, gram.T
 
 

time: 65.3 us -> 64 us (0.980)
  local copies, waits for them, and re-layouts: 2.65 us -> 0 us
  Pallas kernels: 61.8 us -> 63.2 us
    unnamed x2 -> x0, local copies, waits for them, and re-layouts: 2.65 us -> none
    pallas_call x0 -> x1, Pallas kernels: none -> 1.38 us  [body(): pl.pallas_call(settle, out_shape=(jax.ShapeDtypeStruct(product.shape, F32...]
where the time goes in v4:
time: 64 us; the launch traced here: 63.8 us
  Pallas kernels  63.2 us (99%)
  between operations  0.64 us (1%)
    pallas_call x1, Pallas kernels, body(): pl.pallas_call(kernel, out_shape=(jax.ShapeDtypeStruct((COLS, RB * TB), F...  61.8 us
    pallas_call x1, Pallas kernels, body(): pl.pallas_call(settle, out_shape=(jax.ShapeDtypeStruct(product.shape, F32...  1.38 us

profile of v4, /device:TPU:1, one launch (start us, length us, event | category | flops | bytes accessed | tf_op | source)
XLA Modules:
  0.0 63.8 jit_solution(16795239273933159845)
XLA Ops:
  0.6 61.8 %exchange.1 = (f32[8,1024]{1,0:T(8,128)}, f32[8,32]{1,0:T(8,128)}) custom-call(bf16[8,1024]{1,0:T(8,128)(2,1)} %x_hbm.1, s32[8,5]{1,0:T(8,128)} %qc_hbm.1, s32[1,2]{1,0:T(1,128)} %halo_hbm.1, bf16[64,128]{1,0:T(8,128)(2,1)} %prec_hbm.1, s32[1,64]{1,0:T(1,128)} %bitcast.3, s32[1,64]{1,0:T(1,128)} %bitcast.4, bf16[40,128,128]{2,1,0:T(8,128)(2,1)} %q_hbm.1, ...), custom_call_target="tpu_custom_call" | custom-call | tf_op jit(solution)/shard_map/exchange/pallas_call | solution.py:361
  62.4 1.4 %settle.1 = (f32[8,1024]{1,0:T(8,128)}, f32[8,32]{1,0:T(8,128)}) custom-call(f32[8,1024]{1,0:T(8,128)} %get-tuple-element.6.product_ref, f32[8,32]{1,0:T(8,128)} %get-tuple-element.7.gram_ref), custom_call_target="tpu_custom_call" | custom-call | tf_op jit(solution)/shard_map/settle/pallas_call | solution.py:427

commit v5 on v4

--- a/solution.py
+++ b/solution.py
@@ -20,7 +20,8 @@
 SLOTS = 2 * Z
 F32 = jnp.float32
 BF16 = jnp.bfloat16
-GROUP = 8
+GROUP = 32
+LEVELS = 32767.0
 Z_PLAN = [(0, 5, None), (0, -5, None), (0, 1, None), (0, -1, None), (0, 2, None), (0, -2, None)]
 Z_OWN = len(Z_PLAN)
 Z_PLAN += [(-5, 3, 0), (-5, 2, None), (-5, -2, None), (-5, 1, None), (-5, -1, None)]
@@ -38,9 +39,10 @@
     x_hbm, qc_hbm, halo_hbm, prec_hbm, owner_hbm, sub_hbm, q_hbm, a_hbm,
     y_ref, g_ref,
     x_v, qc_s, halo_s, prec_in, own_v, sub_v,
-    q_v, a_v, win, mine, share, zx, zy, xy, req, meta, req_s, meta_s, stage, xs, cb, stage2, rc, dn, near, csum, direct,
+    q_v, a_v, win, mine, share, zx, zy, xy, req, meta, req_s, meta_s, stage, xs, cb, stage2, rc,
+    coded, unit_out, unit_in, dn, near, csum, direct,
     far, acc, g1, g2, gp, prec, pb, wb, pg,
-    loc_sem, s_z, r_z, s_q, r_q, s_y, r_y, s_h, r_h, s_p, r_p, s_c, r_c, s_n, r_n, s_d, r_d, s_f, r_f, s_j, r_j,
+    loc_sem, s_z, r_z, s_q, r_q, s_y, r_y, s_h, r_h, s_p, r_p, s_c, r_c, s_u, r_u, s_n, r_n, s_d, r_d, s_f, r_f, s_j, r_j,
     s_g1, r_g1, s_g2, r_g2,
 ):
     z, x, c, y = (lax.axis_index(n) for n in ("z", "x", "core", "col"))
@@ -235,11 +237,26 @@
             both = lax.dot_general(weighted[i // 2], tiles[i // 2], NN, preferred_element_type=F32)
             cb[base + i] = both[:COLS]
             cb[base + i + 1] = both[COLS:]
+            carry = jnp.maximum(carry, jnp.maximum(jnp.abs(both[:COLS]), jnp.abs(both[COLS:])))
         return carry
 
-    lax.fori_loop(0, TILES // GROUP, terms, 0)
-    cb[TILES] = jnp.zeros((COLS, TB), F32)
+    largest = lax.fori_loop(0, TILES // GROUP, terms, jnp.zeros((COLS, TB), F32))
     turns = start([send(pb, pg.at[y], (s_j, r_j), d, at_y(d)) for d in range(1, Y)])
+
+    largest = jnp.broadcast_to(jnp.max(largest, axis=1, keepdims=True), (COLS, TB))
+    unit_out[...] = largest * (1.0 / LEVELS)
+    unit_in[mq] = unit_out[...]
+    units = start([send(unit_out, unit_in.at[mq], (s_u, r_u), k, plane_peer(k)[0]) for k in range(1, PLANE)])
+    per_unit = LEVELS / jnp.maximum(largest, 1e-30)
+
+    def code(group, carry):
+        for i in range(GROUP):
+            t = group * GROUP + i
+            coded[t] = jnp.floor(cb[t] * per_unit + 0.5).astype(jnp.int32).astype(jnp.int16)
+        return carry
+
+    lax.fori_loop(0, TILES // GROUP, code, 0)
+    coded[TILES] = jnp.zeros((COLS, TB), jnp.int16)
 
     def back(wave, k):
         low, high = WAVES[wave]
@@ -249,7 +266,7 @@
     def place(wave, k, dst):
         _, q = plane_peer(k)
         for i in range(2 * WAVES[wave][0], 2 * WAVES[wave][1]):
-            dst[i] = cb[meta_s[PLANE + q, i]]
+            dst[i] = coded[meta_s[PLANE + q, i]]
 
     for wave in (1, 0):
 
@@ -275,30 +292,13 @@
         return carry
 
     lax.fori_loop(0, RB, prior, 0, unroll=4)
-    finish(probes)
-    part = jnp.zeros((COLS, COLS * Y), F32)
-    for r in range(RB):
-        across = jnp.concatenate([xy[i, :, r * TB:(r + 1) * TB] for i in range(Y)], axis=0)
-        part += lax.dot_general(
-            acc[r], across.astype(F32), NT, precision=lax.Precision.HIGHEST, preferred_element_type=F32)
-    finish(turns)
-
-    def gram_part(i, part):
-        lanes = pl.ds(pl.multiple_of(i * 1024, 1024), 1024)
-        across = jnp.concatenate([pg[j, :, lanes] for j in range(Y)], axis=0)
-        return part + lax.dot_general(wb[:, lanes], across, NT, preferred_element_type=F32)
-
-    part = lax.fori_loop(0, TILES * TB // 1024, gram_part, part)
-    gp[...] = jnp.concatenate([part[2 * i:2 * i + 2] for i in range(COLS // 2)], axis=1)
-    firsts = start([send(gp, g1.at[k], (s_g1, r_g1), k, plane_peer(k)[0]) for k in range(1, PLANE)])
-    g1[0] = gp[...]
-
     def dense(i, carry):
         totals = [jnp.zeros((COLS, TB), F32) for _ in range(RB)]
         for q in range(PLANE):
+            unit = unit_in[q]
             for j in range(2):
                 sub = jnp.broadcast_to(req_s[q, mq, 2 * i + j], (COLS, TB))
-                block = rc[q, 2 * i + j]
+                block = rc[q, 2 * i + j].astype(jnp.int32).astype(F32) * unit
                 totals = [total + jnp.where(sub == r, block, 0.0) for r, total in enumerate(totals)]
         for r in range(RB):
             dn[i, r] = totals[r]
@@ -307,6 +307,7 @@
     def sums_for(d):
         return dn.at[ORDER.index(d % Z)]
 
+    finish(units)
     finish([back(1, k) for k in range(1, PLANE)])
     lax.fori_loop(*WAVES[1], dense, 0)
     nears = []
@@ -316,12 +317,30 @@
             rows = pl.ds(half * (RB // 2), RB // 2)
             src, dst = src.at[rows], dst.at[rows]
         nears += start([send(src, dst, (s_n, r_n), i, at_z(step))])
+    finish(probes)
+    part = jnp.zeros((COLS, COLS * Y), F32)
+    for r in range(RB):
+        across = jnp.concatenate([xy[i, :, r * TB:(r + 1) * TB] for i in range(Y)], axis=0)
+        part += lax.dot_general(
+            acc[r], across.astype(F32), NT, precision=lax.Precision.HIGHEST, preferred_element_type=F32)
+    finish(turns)
+
+    def gram_part(i, part):
+        lanes = pl.ds(pl.multiple_of(i * 1024, 1024), 1024)
+        across = jnp.concatenate([pg[j, :, lanes] for j in range(Y)], axis=0)
+        return part + lax.dot_general(wb[:, lanes], across, NT, preferred_element_type=F32)
+
+    part = lax.fori_loop(0, TILES * TB // 1024, gram_part, part)
+    gp[...] = jnp.concatenate([part[2 * i:2 * i + 2] for i in range(COLS // 2)], axis=1)
+    firsts = start([send(gp, g1.at[k], (s_g1, r_g1), k, plane_peer(k)[0]) for k in range(1, PLANE)])
+    g1[0] = gp[...]
+
+    finish([back(0, k) for k in range(1, PLANE)])
+    lax.fori_loop(*WAVES[0], dense, 0)
+    directs = start([send(sums_for(d), direct.at[i], (s_d, r_d), i, at_z(d)) for i, d in enumerate((1, -1, 2, -2))])
     finish(firsts)
     g2[0] = jnp.sum(g1[...], axis=0)
     seconds = start([send(g2.at[0], g2.at[d], (s_g2, r_g2), d, at_z(d)) for d in range(1, Z)])
-    finish([back(0, k) for k in range(1, PLANE)])
-    lax.fori_loop(*WAVES[0], dense, 0)
-    directs = start([send(sums_for(d), direct.at[i], (s_d, r_d), i, at_z(d)) for i, d in enumerate((1, -1, 2, -2))])
     finish(nears)
     fars = []
     for g, d in enumerate((-5, 5)):
@@ -387,9 +406,12 @@
             pltpu.SMEM((2 * PLANE, TB), jnp.int32),
             pltpu.VMEM((PLANE, SLOTS, *block), BF16),
             pltpu.VMEM((PLANE, SLOTS, *block), BF16),
-            pltpu.VMEM((TILES + 1, *block), F32),
-            pltpu.VMEM((PLANE, SLOTS, *block), F32),
-            pltpu.VMEM((PLANE, SLOTS, *block), F32),
+            pltpu.VMEM((TILES, *block), F32),
+            pltpu.VMEM((PLANE, SLOTS, *block), jnp.int16),
+            pltpu.VMEM((PLANE, SLOTS, *block), jnp.int16),
+            pltpu.VMEM((TILES + 1, *block), jnp.int16),
+            pltpu.VMEM(block, F32),
+            pltpu.VMEM((PLANE, *block), F32),
             pltpu.VMEM((Z, RB, *block), F32),
             pltpu.VMEM((len(N_PLAN), RB, *block), F32),
             pltpu.VMEM((2, RB, *block), F32),
@@ -410,6 +432,7 @@
             *pair(4),
             *pair(2, PLANE),
             *pair(2, PLANE),
+            *pair(PLANE),
             *pair(len(N_PLAN)),
             *pair(4),
             *pair(2),

time: 64 us -> 59.3 us (0.927)
  Pallas kernels: 63.2 us -> 58.5 us
    pallas_call x1, Pallas kernels: 61.8 us -> 57.1 us  [body(): pl.pallas_call(kernel, out_shape=(jax.ShapeDtypeStruct((COLS, RB * TB), F...]
where the time goes in v5:
time: 59.3 us; the launch traced here: 59.1 us
  Pallas kernels  58.5 us (99%)
  between operations  0.64 us (1%)
    pallas_call x1, Pallas kernels, body(): pl.pallas_call(kernel, out_shape=(jax.ShapeDtypeStruct((COLS, RB * TB), F...  57.1 us
    pallas_call x1, Pallas kernels, body(): pl.pallas_call(settle, out_shape=(jax.ShapeDtypeStruct(product.shape, F32...  1.38 us

profile of v5, /device:TPU:1, one launch (start us, length us, event | category | flops | bytes accessed | tf_op | source)
XLA Modules:
  0.0 59.1 jit_solution(17122275741609550058)
XLA Ops:
  0.6 57.1 %exchange.1 = (f32[8,1024]{1,0:T(8,128)}, f32[8,32]{1,0:T(8,128)}) custom-call(bf16[8,1024]{1,0:T(8,128)(2,1)} %x_hbm.1, s32[8,5]{1,0:T(8,128)} %qc_hbm.1, s32[1,2]{1,0:T(1,128)} %halo_hbm.1, bf16[64,128]{1,0:T(8,128)(2,1)} %prec_hbm.1, s32[1,64]{1,0:T(1,128)} %bitcast.3, s32[1,64]{1,0:T(1,128)} %bitcast.4, bf16[40,128,128]{2,1,0:T(8,128)(2,1)} %q_hbm.1, ...), custom_call_target="tpu_custom_call" | custom-call | tf_op jit(solution)/shard_map/exchange/pallas_call | solution.py:380
  57.7 1.4 %settle.1 = (f32[8,1024]{1,0:T(8,128)}, f32[8,32]{1,0:T(8,128)}) custom-call(f32[8,1024]{1,0:T(8,128)} %get-tuple-element.6.product_ref, f32[8,32]{1,0:T(8,128)} %get-tuple-element.7.gram_ref), custom_call_target="tpu_custom_call" | custom-call | tf_op jit(solution)/shard_map/settle/pallas_call | solution.py:450

commit v6 on v5

--- a/solution.py
+++ b/solution.py
@@ -20,7 +20,7 @@
 SLOTS = 2 * Z
 F32 = jnp.float32
 BF16 = jnp.bfloat16
-GROUP = 32
+GROUP = 64
 LEVELS = 32767.0
 Z_PLAN = [(0, 5, None), (0, -5, None), (0, 1, None), (0, -1, None), (0, 2, None), (0, -2, None)]
 Z_OWN = len(Z_PLAN)

time: 59.3 us -> 59.3 us (level)
  no operation moved by 1% of the time
where the time goes in v6:
time: 59.3 us; the launch traced here: 59.1 us
  Pallas kernels  58.4 us (98%)
  between operations  0.64 us (1%)
    pallas_call x1, Pallas kernels, body(): pl.pallas_call(kernel, out_shape=(jax.ShapeDtypeStruct((COLS, RB * TB), F...  57.1 us
    pallas_call x1, Pallas kernels, body(): pl.pallas_call(settle, out_shape=(jax.ShapeDtypeStruct(product.shape, F32...  1.38 us

profile of v6, /device:TPU:1, one launch (start us, length us, event | category | flops | bytes accessed | tf_op | source)
XLA Modules:
  0.0 59.1 jit_solution(501470320020733269)
XLA Ops:
  0.6 57.1 %exchange.1 = (f32[8,1024]{1,0:T(8,128)}, f32[8,32]{1,0:T(8,128)}) custom-call(bf16[8,1024]{1,0:T(8,128)(2,1)} %x_hbm.1, s32[8,5]{1,0:T(8,128)} %qc_hbm.1, s32[1,2]{1,0:T(1,128)} %halo_hbm.1, bf16[64,128]{1,0:T(8,128)(2,1)} %prec_hbm.1, s32[1,64]{1,0:T(1,128)} %bitcast.3, s32[1,64]{1,0:T(1,128)} %bitcast.4, bf16[40,128,128]{2,1,0:T(8,128)(2,1)} %q_hbm.1, ...), custom_call_target="tpu_custom_call" | custom-call | tf_op jit(solution)/shard_map/exchange/pallas_call | solution.py:380
  57.7 1.4 %settle.1 = (f32[8,1024]{1,0:T(8,128)}, f32[8,32]{1,0:T(8,128)}) custom-call(f32[8,1024]{1,0:T(8,128)} %get-tuple-element.6.product_ref, f32[8,32]{1,0:T(8,128)} %get-tuple-element.7.gram_ref), custom_call_target="tpu_custom_call" | custom-call | tf_op jit(solution)/shard_map/settle/pallas_call | solution.py:450
